TPU v7x, 256 devices: a whole 4x4x8 slice. The times are simulated.
256 devices in a mesh: tok: 4 (over z_hi), voc: 64 (over z_lo, y, x, core).
Axes of the slice: x: 4, y: 4, z: 8 (z_hi: 4, z_lo: 2; z = z_hi * 2 + z_lo), core: 2. Of those that a mesh axis runs over, the one named last changes fastest.
Arguments:
- hidden: bfloat16 [512, 3584], P('tok'), may hold values from -15 to 15
- valid_mask: int32 [512], P('tok'), may hold values from 0 to 1, as said below
- student_head: bfloat16 [192000, 3584], P(('voc', 'tok')), may hold values from -0.09375 to 0.09375
- teacher_logits: bfloat16 [512, 192000], P('tok', 'voc'), may hold values from -12 to 12
Outputs:
- token_kl: float32 [512], P('tok')
- d_hidden: bfloat16 [512, 3584], P('tok', 'voc')
- d_head: bfloat16 [192000, 3584], P(('voc', 'tok'))
Inputs may be any that keep to these rules, and one draw needn't show every extreme that they name: `valid_mask`: the last token of every block of 128 tokens is valid, and in at least one such block every token is valid.
All inputs are finite; a program needn't handle non-finite values.
Results may differ from a plain program's by a relative error of at most 0.005.
Values may be sent and summed in bfloat16 or wider, within the bound.
A program may use at most 64 MiB of HBM per device.

v0:
```python
import jax
import jax.numpy as jnp
from jax import lax
from jax.sharding import PartitionSpec as P

CAP = 30.0


def on_device(hidden, valid_mask, student_head, teacher_logits):
    row_count = hidden.shape[0]
    all_hidden, all_valid = (
        lax.all_gather(hidden, "tok", axis=0, tiled=True),
        lax.all_gather(valid_mask.astype(jnp.bfloat16), "tok", axis=0, tiled=True),
    )
    target = lax.all_to_all(teacher_logits, "tok", split_axis=1, concat_axis=0, tiled=True).astype(
        jnp.float32
    )
    teacher_exp = jnp.exp(target)
    raw_logits = lax.dot_general(
        all_hidden, student_head, (((1,), (1,)), ((), ())), preferred_element_type=jnp.float32
    )
    capped = CAP * jnp.tanh(raw_logits / CAP)
    student_exp = jnp.exp(capped)
    cross_part = jnp.sum(teacher_exp * (target - capped), axis=1)
    student_total, teacher_total, cross = lax.psum(
        (jnp.sum(student_exp, axis=1), jnp.sum(teacher_exp, axis=1), cross_part), ("tok", "voc")
    )
    all_kl = cross / teacher_total - jnp.log(teacher_total) + jnp.log(student_total)
    token_kl = lax.dynamic_slice_in_dim(all_kl, lax.axis_index("tok") * row_count, row_count, 0)
    mask_float = all_valid.astype(jnp.float32)
    token_count = jnp.sum(mask_float)
    loss_scale = all_hidden.shape[0] / token_count
    row_weight = loss_scale * mask_float
    grad = row_weight[:, None] * (
        student_exp / student_total[:, None] - teacher_exp / teacher_total[:, None]
    )
    grad = (grad * (1.0 - (capped / CAP) ** 2)).astype(jnp.bfloat16)
    head_grad = lax.dot_general(
        grad, all_hidden, (((0,), (0,)), ((), ())), preferred_element_type=jnp.float32
    )
    partial_grad = jnp.dot(grad, student_head, preferred_element_type=jnp.float32)
    by_features = lax.psum_scatter(partial_grad, "voc", scatter_dimension=1, tiled=True)
    grad_hidden = lax.psum_scatter(by_features, "tok", scatter_dimension=0, tiled=True)
    return (token_kl, grad_hidden.astype(jnp.bfloat16), head_grad.astype(jnp.bfloat16))


def solution(mesh):
    return jax.shard_map(
        on_device,
        mesh=mesh,
        in_specs=(P("tok", None), P("tok"), P(("voc", "tok"), None), P("tok", "voc")),
        out_specs=(P("tok"), P("tok", "voc"), P(("voc", "tok"), None)),
        check_vma=False,
    )
```

profile of v0, /device:TPU:1, one launch (start us, length us, event | category | flops | bytes accessed | tf_op | source)
XLA Modules:
  0.0 517.1 jit_solution(7836584749235676762)
XLA Ops:
  7.2 0.0 all-gather.3.cloned.1.call-start
  7.2 0.7 all-gather.3.cloned.1.call-update
  7.9 0.0 copy-start
  7.9 2.2 all_to_all.10
  10.1 9.0 %all-to-all-start = ((bf16[128,4,750]{0,2,1:T(8,128)(2,1)}), bf16[128,4,750]{0,2,1:T(8,128)(2,1)S(1)}, u32[]{:S(2)}, u32[]{:S(2)}) async-start(bf16[128,4,750]{0,2,1:T(8,128)(2,1)} %all_to_all.10), calls=%async_computation | async-start | bytes 1540096 | tf_op jit(solution)/shard_map/all_to_all | solution.py:15
  19.1 0.0 reduce-scatter.3.cloned.1.call-start
  19.1 0.0 copy-done
  19.1 28.5 %all-gather = bf16[4,1,128]{2,1,0:T(2,128)(2,1)S(1)} all-gather(bf16[1,1,128]{2,1,0:T(2,128)(2,1)S(1)} %convert_bitcast_fusion.1), channel_id=1, replica_groups=mesh['tok'=4,'voc'=64] {'tok'}, dimensions={0}, use_global_device_ids=true | all-gather | bytes 1280 | tf_op jit(solution)/shard_map/all_gather | solution.py:13
  47.7 0.6 convert_reduce_fusion
  49.0 0.0 all-to-all-done
  49.0 0.1 convert_bitcast_fusion
  49.1 0.6 copy.12
  49.7 0.3 pad
  50.0 0.1 copy.10
  50.1 0.2 fusion
  50.3 45.1 %all-gather.3.cloned.1.call-done = bf16[512,3584]{1,0:T(8,128)(2,1)} async-done(((bf16[128,3584]{1,0:T(8,128)(2,1)}), bf16[512,3584]{1,0:T(8,128)(2,1)}) %all-gather.3.cloned.1.call-update) | async-done | bytes 3670032 | tf_op jit(solution)/shard_map/all_gather | solution.py:12
  95.4 8.2 %multiply_reduce_fusion = (f32[512]{0:T(512)S(1)}, f32[512]{0:T(512)S(1)}, f32[512,750]{0,1:T(8,128)}) fusion(f32[512,750]{0,1:T(8,128)S(1)} %bitcast.23, bf16[512,3584]{1,0:T(8,128)(2,1)} %all-gather.3.cloned.1.call-done, bf16[750,3584]{1,0:T(8,128)(2,1)} %param.6), kind=kOutput, calls=%fused_computation.5 | convolution fusion | flops 2754814976 | bytes 12122112 | tf_op jit(solution)/shard_map/dot_general | solution.py:19
  103.6 81.4 %all-reduce = (f32[512]{0:T(512)S(1)}, f32[512]{0:T(512)S(1)}, f32[512]{0:T(512)S(1)}) all-reduce(f32[512]{0:T(512)S(1)} %get-tuple-element.4, f32[512]{0:T(512)S(1)} %bitcast.26, f32[512]{0:T(512)S(1)} %get-tuple-element.3), channel_id=1, replica_groups=mesh['tok'=4,'voc'=64] {'tok','voc'}, use_global_device_ids=true, to_apply=%region_5.0 | all-reduce | flops 1536 | bytes 12288 | tf_op jit(solution)/shard_map/psum | solution.py:25
  185.0 9.2 %fusion.1 = f32[512,3584]{0,1:T(8,128)} fusion(bf16[750,3584]{1,0:T(8,128)(2,1)} %param.6, f32[512,750]{0,1:T(8,128)} %get-tuple-element.8, f32[512,750]{0,1:T(8,128)S(1)} %bitcast.24, f32[512]{0:T(512)S(1)} %get-tuple-element.6, f32[512]{0:T(512)S(1)} %get-tuple-element.5, f32[512]{0:T(512)S(1)} %bitcast.27), kind=kOutput, calls=%fused_computation.13 | convolution fusion | flops 2755968000 | bytes 15794176 | tf_op jit(solution)/shard_map/dot_general | solution.py:41
  194.2 0.0 copy-start.1
  194.2 0.0 reduce-scatter.3.cloned.1.call-update
  194.3 0.0 reduce-scatter.5.cloned.1.call-start
  194.3 287.3 %reduce-scatter.3.cloned.1.call-done = f32[512,56]{0,1:T(8,128)} async-done(((f32[512,3584]{0,1:T(8,128)}), f32[512,56]{0,1:T(8,128)}) %reduce-scatter.3.cloned.1.call-update) | async-done | bytes 114704 | tf_op jit(solution)/shard_map/reduce_scatter | solution.py:42
  481.6 0.0 reduce-scatter.5.cloned.1.call-update
  481.6 0.0 copy-done.1
  481.6 7.0 %convolution_convert_fusion = bf16[750,3584]{1,0:T(8,128)(2,1)} fusion(bf16[512,3584]{1,0:T(8,128)(2,1)} %all-gather.3.cloned.1.call-done, f32[512,750]{0,1:T(8,128)S(1)} %copy-done.1, f32[512,750]{0,1:T(8,128)S(1)} %bitcast.25, f32[512]{0:T(512)S(1)} %get-tuple-element.6, f32[512]{0:T(512)S(1)} %get-tuple-element.5, f32[512]{0:T(512)S(1)} %bitcast.28), kind=kOutput, calls=%fused_computation | convolution fusion | flops 2758656000 | bytes 12124160 | tf_op jit(solution)/shard_map/dot_general | solution.py:38
  488.6 0.6 dynamic_slice.3
  489.2 20.0 %reduce-scatter.5.cloned.1.call-done = f32[128,56]{0,1:T(8,128)} async-done(((f32[512,56]{0,1:T(8,128)}), f32[128,56]{0,1:T(8,128)}) %reduce-scatter.5.cloned.1.call-update) | async-done | bytes 28688 | tf_op jit(solution)/shard_map/reduce_scatter | solution.py:43
  509.2 1.3 convert_element_type.35
  (3 shorter events, 0.0 us)
Async XLA Ops:
  7.2 88.2 %all-gather.3.cloned.1.call-start = ((), (), s32[]{:S(2)}) async-start(), calls=%async_computation.3 | async-start | bytes 4587520 | tf_op jit(solution)/shard_map/all_gather | solution.py:12
  7.9 11.2 %copy-start = (s32[128]{0:T(128)S(1)}, s32[128]{0:T(128)}, u32[]{:S(2)}) copy-start(s32[128]{0:T(128)} %param.5) | copy-start | bytes 1540
  10.1 38.9 %all-to-all-start = ((bf16[128,4,750]{0,2,1:T(8,128)(2,1)}), bf16[128,4,750]{0,2,1:T(8,128)(2,1)S(1)}, u32[]{:S(2)}, u32[]{:S(2)}) async-start(bf16[128,4,750]{0,2,1:T(8,128)(2,1)} %all_to_all.10), calls=%async_computation | async-start | bytes 1540096 | tf_op jit(solution)/shard_map/all_to_all | solution.py:15
  19.1 462.5 %reduce-scatter.3.cloned.1.call-start = ((), (), s32[]{:S(2)}) async-start(), calls=%async_computation.4 | async-start | bytes 7454720 | tf_op jit(solution)/shard_map/reduce_scatter | solution.py:42
  194.2 287.4 %copy-start.1 = (f32[512,750]{0,1:T(8,128)S(1)}, f32[512,750]{0,1:T(8,128)}, u32[]{:S(2)}) copy-start(f32[512,750]{0,1:T(8,128)} %get-tuple-element.8) | copy-start | bytes 4608004
  194.3 315.0 %reduce-scatter.5.cloned.1.call-start = ((), (), s32[]{:S(2)}) async-start(), calls=%async_computation.5 | async-start | bytes 143360 | tf_op jit(solution)/shard_map/reduce_scatter | solution.py:43
Sparse Core Ops, SparseCore 0:
  9.8 85.5 all-gather.2
  194.4 287.1 reduce-scatter.2
  484.3 24.9 reduce-scatter.4
where the time goes:
time: 519 us; the launch traced here: 517 us
  waiting for transfers between devices  353 us (68%)
  blocking collectives  110 us (21%)
  matrix products  24.4 us (5%)
  between operations  14.5 us (3%)
  starting transfers between devices  9.09 us (2%)
    reduce_scatter x1, waiting for transfers between devices, on_device(): lax.psum_scatter(partial_grad, 'voc', scatter_dimension=1, tiled=True)  287 us
    psum x1, blocking collectives, on_device(): lax.psum((jnp.sum(student_exp, axis=1), jnp.sum(teacher_exp, axis=1), cro...  81.4 us
    all_gather x1, waiting for transfers between devices, on_device(): lax.all_gather(hidden, 'tok', axis=0, tiled=True)  45.1 us
    all_gather x1, blocking collectives, on_device(): lax.all_gather(valid_mask.astype(jnp.bfloat16), 'tok', axis=0, tiled=True)  28.5 us
    reduce_scatter x1, waiting for transfers between devices, on_device(): lax.psum_scatter(by_features, 'tok', scatter_dimension=0, tiled=True)  20 us
  transfers between devices with their start and end apart: 4, of which 3 were waited for; matrix products, arithmetic and copies ran while one was open for 2% of the time, Pallas kernels for 0%

commit v1 on v0

v1 whole, which is shorter than its diff:
```python
import jax
import jax.numpy as jnp
from jax import lax
from jax.experimental import pallas as pl
from jax.experimental.pallas import tpu as pltpu
from jax.sharding import PartitionSpec as P

CAP = 30.0
D = 3584
ROWS = 128
HALF = 256
SLAB = 750
VP = 768
QCOL = D // 4
PIECE = ROWS // 4
CHIPCOL = 112
MESH = pl.DeviceIdType.MESH
F32 = jnp.float32
BF16 = jnp.bfloat16


def kernel(
    hid, mask, head, teach, kl_out, dhid_out, DH,
    H, HD, HDT, EYE, tin, TS, TR, RLY, TSIB, CP, ES, GV, GTD,
    TT, TG1, TT2, TG2, TOT, AL, BE, CR, CG1, CR2, CG2, KL,
    OWN, NEXT, B1, R1, F1, B2, R2, B3, RZ,
    local, hs, hr, zs, zr, p1s, p1r, p2s, p2r, cs, cr, ts, tr, gs, gr,
    as1, ar1, as2, ar2, bs1, br1, bs2, br2, q1s, q1r, q2s, q2r, rzs, rzr,
):
    a = lax.axis_index("tok")
    v = lax.axis_index("voc")
    c = lax.rem(v, 2)
    x = lax.rem(v // 2, 4)
    y = lax.rem(v // 8, 4)
    zl = v // 32
    z = 2 * a + zl
    p = jnp.where(c == 0, x, y)
    q = jnp.where(c == 0, y, x)

    def dev(a_, zl_, y_, x_, c_):
        return (a_, zl_ * 32 + y_ * 8 + x_ * 2 + c_)

    def at_p(p_):
        return dev(a, zl, jnp.where(c == 0, y, p_), jnp.where(c == 0, p_, x), c)

    def at_q(q_):
        return dev(a, zl, jnp.where(c == 0, q_, y), jnp.where(c == 0, x, q_), c)

    sib = dev(a, zl, y, x, 1 - c)

    def at_a(a_):
        return dev(a_, zl, y, x, c)

    def at_xy(k):
        return dev(a, zl, k // 4, lax.rem(k, 4), c)

    def at_zc(k):
        return dev(k // 4, lax.rem(k // 2, 2), y, x, lax.rem(k, 2))

    def mod4(k):
        return lax.rem(k + 8, 4)

    me_xy = y * 4 + x
    me_zc = z * 2 + c

    pending = []

    def send(src, dst, ssem, rsem, to):
        copy = pltpu.make_async_remote_copy(
            src_ref=src, dst_ref=dst, send_sem=ssem, recv_sem=rsem, device_id=to, device_id_type=MESH
        )
        copy.start()
        pending.append(copy)

    def arrived(dst, ssem, rsem):
        pltpu.make_async_remote_copy(
            src_ref=dst, dst_ref=dst, send_sem=ssem, recv_sem=rsem, device_id=sib, device_id_type=MESH
        ).wait_recv()

    load_teach = pltpu.make_async_copy(teach, tin, local.at[0])
    load_teach.start()
    load_hid = pltpu.make_async_copy(hid, H.at[pl.ds(0, ROWS)], local.at[1])
    load_hid.start()
    load_head = pltpu.make_async_copy(head, DH, local.at[2])
    load_head.start()

    barrier = pltpu.get_barrier_semaphore()
    for k in range(1, 16):
        pl.semaphore_signal(barrier, inc=1, device_id=at_xy(lax.rem(me_xy + k, 16)), device_id_type=MESH)
        pl.semaphore_signal(barrier, inc=1, device_id=at_zc(lax.rem(me_zc + k, 16)), device_id_type=MESH)
    pl.semaphore_wait(barrier, 30)

    def span(start, size):
        return pl.ds(pl.multiple_of(start, 16), size)

    def cols(q_):
        return pl.ds(pl.multiple_of(q_ * QCOL, 128), QCOL)

    def base(g):
        return ROWS + c * ROWS + g * ROWS

    later = []

    def each_group(step):
        step(0)

        @pl.when(c == 1)
        def _():
            step(1)

    def send_group(g, make):
        copy = make(g)
        copy.start()
        if g == 0:
            pending.append(copy)
        else:
            later.append(lambda: make(1))

    def remote(src, dst, ssem, rsem, to):
        return pltpu.make_async_remote_copy(
            src_ref=src, dst_ref=dst, send_sem=ssem, recv_sem=rsem, device_id=to, device_id_type=MESH
        )

    each_group(lambda g: send_group(g, lambda g: remote(
        hid.at[span(p * PIECE, PIECE), cols(q)], H.at[span(base(g) + p * PIECE, PIECE), cols(q)],
        zs.at[g], zr.at[g], at_a(mod4(a - 1 - c - g)),
    )))

    load_teach.wait()
    place = lax.broadcasted_iota(jnp.int32, (VP, ROWS), 0)
    teacher_sum = jnp.zeros((1, ROWS), F32)
    for t in range(4):
        start = t * SLAB // 16 * 16
        off = t * SLAB - start
        height = min(VP + 16, 3000 - start)
        tall = tin[start : start + height].astype(F32)
        if height < VP + 16:
            tall = jnp.concatenate([tall, jnp.zeros((VP + 16 - height, ROWS), F32)], axis=0)
        if off:
            tall = pltpu.roll(tall, VP + 16 - off, 0)
        part = jnp.where(place < SLAB, tall[:VP], -30000.0)
        TS[t] = part.astype(BF16)
        teacher_sum = teacher_sum + jnp.sum(jnp.exp(part), axis=0, keepdims=True)
    way = jnp.where(c == 0, 1, 3)
    send(TS.at[mod4(a + 2)], RLY, ts.at[2], tr.at[2], at_a(mod4(a + way)))
    send(TS.at[mod4(a + 1)], TR.at[3], ts.at[0], tr.at[0], at_a(mod4(a + 1)))
    send(TS.at[mod4(a + 3)], TR.at[1], ts.at[1], tr.at[1], at_a(mod4(a + 3)))
    TR[0] = TS[a]

    TT[...] = jnp.zeros_like(TT)
    TT[pl.ds(4 + a, 1)] = teacher_sum
    TT[pl.ds(8 + a, 1)] = mask[...].astype(F32)

    nt = (((1,), (1,)), ((), ()))
    EYE[...] = jnp.where(
        lax.broadcasted_iota(jnp.int32, (256, 256), 0) == lax.broadcasted_iota(jnp.int32, (256, 256), 1), 1.0, 0.0
    ).astype(BF16)

    def turn(slab, half):
        for n in range(7):
            at = pl.ds(half * 1792 + n * 256, 256)
            out = lax.dot_general(
                EYE[...], HD[slab * VP : (slab + 1) * VP, at], nt, preferred_element_type=F32
            ).astype(BF16)
            done = 0
            while done < 256:
                chip, row = divmod(n * 256 + done, CHIPCOL)
                size = min(CHIPCOL - row, 256 - done)
                HDT[half, chip // 4, chip % 4, row : row + size, slab * VP : (slab + 1) * VP] = out[done : done + size]
                done += size

    def piece(g, p_):
        return H.at[span(base(g) + p_ * PIECE, PIECE), cols(q)]

    def first_step(g):
        arrived(piece(g, p), zs.at[g], zr.at[g])
        for d in range(1, 4):
            send_group(g, lambda g, d=d: remote(
                piece(g, p), piece(g, p), p1s.at[g, d - 1], p1r.at[g, d - 1], at_p(mod4(p + d)),
            ))

    each_group(first_step)

    load_head.wait()
    for k in range(3):
        if k == 2:
            HD[736:768] = jnp.concatenate([DH[736:750].astype(F32), jnp.zeros((18, D), F32)], axis=0).astype(BF16)

        @pl.loop(k * 8, min(k * 8 + 8, 23))
        def _(i):
            HD[pl.ds(pl.multiple_of(i * 32, 32), 32)] = DH[pl.ds(pl.multiple_of(i * 32, 32), 32)]

        send(HD.at[k * 256 : (k + 1) * 256], HD.at[VP + k * 256 : VP + (k + 1) * 256], hs.at[k], hr.at[k], sib)

    def first_end(g):
        for d in range(1, 4):
            arrived(piece(g, mod4(p - d)), p1s.at[g, d - 1], p1r.at[g, d - 1])

    each_group(first_end)

    right, left = at_q(mod4(q + 1)), at_q(mod4(q - 1))
    before, after, across = mod4(q - 1), mod4(q + 1), mod4(q + 2)

    def part_of(g, half, q_):
        return H.at[span(base(g) + half * 64, 64), cols(q_)]

    def pass_on(n, half, q_, to):
        each_group(lambda g: send_group(g, lambda g: remote(
            part_of(g, half, q_), part_of(g, half, q_), p2s.at[g, n], p2r.at[g, n], to,
        )))

    def passed(n, half, q_):
        each_group(lambda g: arrived(part_of(g, half, q_), p2s.at[g, n], p2r.at[g, n]))

    my_half = pl.ds(pl.multiple_of(c * HALF, HALF), HALF)

    def logits(slab, q_, first=False):
        rr = slice(slab * VP, (slab + 1) * VP)
        out = lax.dot_general(HD[rr, cols(q_)], H[my_half, cols(q_)], nt, preferred_element_type=F32)
        CP[rr] = out if first else CP[rr] + out

    pass_on(0, 0, q, right)
    pass_on(1, 1, q, left)
    pass_on(2, 1, q, right)
    pass_on(3, 0, q, left)
    load_hid.wait()
    logits(0, q, True)
    turn(0, 0)
    passed(0, 0, before)
    pass_on(4, 0, before, right)
    passed(1, 1, after)
    pass_on(5, 1, after, left)
    turn(0, 1)
    passed(2, 1, before)
    logits(0, before)
    passed(3, 0, after)
    logits(0, after)
    for k in range(3):
        arrived(HD.at[VP + k * 256 : VP + (k + 1) * 256], hs.at[k], hr.at[k])
    logits(1, q, True)
    logits(1, before)
    logits(1, after)
    passed(4, 0, across)
    passed(5, 1, across)
    logits(0, across)
    logits(1, across)

    arrived(RLY, ts.at[2], tr.at[2])
    send(RLY, TR.at[2], ts.at[3], tr.at[3], at_a(mod4(a + way)))

    def share(g):
        return H.at[span(base(g), ROWS)]

    each_group(lambda g: send_group(g, lambda g: remote(share(g), share(g), cs.at[g], cr.at[g], sib)))

    in_slab = lax.broadcasted_iota(jnp.int32, (256, HALF), 0) < SLAB - 512
    student_sum = jnp.zeros((1, HALF), F32)
    for k in range(6):
        rr = slice(k * 256, (k + 1) * 256)
        capped = CAP * jnp.tanh(CP[rr] * (1.0 / CAP))
        exps = jnp.exp(capped)
        if k % 3 == 2:
            exps = jnp.where(in_slab, exps, 0.0)
        CP[rr] = capped
        ES[rr] = exps
        student_sum = student_sum + jnp.sum(exps, axis=0, keepdims=True)
    my_rows = (mod4(a + 2 * c), mod4(a + 2 * c + 1))
    for i in range(2):
        TT[pl.ds(my_rows[i], 1)] = student_sum[:, i * 128 : (i + 1) * 128]

    def exchange_start(tile, slots, ssem, rsem, me, at):
        for k in range(1, 16):
            send(tile, slots.at[me], ssem.at[k - 1], rsem.at[k - 1], at(lax.rem(me + k, 16)))

    def exchange_end(tile, slots, ssem, rsem, me):
        slots[me] = tile[...]
        for k in range(1, 16):
            arrived(slots.at[lax.rem(me + 16 - k, 16)], ssem.at[k - 1], rsem.at[k - 1])
        total = slots[0]
        for k in range(1, 16):
            total = total + slots[k]
        return total

    exchange_start(TT, TG1, as1, ar1, me_xy, at_xy)

    def factors(slab, cross_sum):
        for k in range(6):
            rr = slice(slab * VP + k * 128, slab * VP + (k + 1) * 128)
            vv = slice(k * 128, (k + 1) * 128)
            if slab == 0:
                target = jnp.concatenate([TR[2 * c, vv], TR[2 * c + 1, vv]], axis=1).astype(F32)
            else:
                target = jnp.concatenate([TSIB[0, vv], TSIB[1, vv]], axis=1).astype(F32)
            expd = jnp.exp(target)
            capped = CP[rr]
            cross_sum = cross_sum + jnp.sum(expd * (target - capped), axis=0, keepdims=True)
            ratio = capped * (1.0 / CAP)
            slope = 1.0 - ratio * ratio
            ES[rr] = ES[rr] * slope
            CP[rr] = expd * slope
        return cross_sum

    turn(1, 0)
    TT2[...] = exchange_end(TT, TG1, as1, ar1, me_xy)
    exchange_start(TT2, TG2, as2, ar2, me_zc, at_zc)
    arrived(TR.at[3], ts.at[0], tr.at[0])
    arrived(TR.at[1], ts.at[1], tr.at[1])
    arrived(TR.at[2], ts.at[3], tr.at[3])
    send(TR.at[pl.ds(2 * (1 - c), 2)], TSIB, ts.at[4], tr.at[4], sib)
    cross_sum = factors(0, jnp.zeros((1, HALF), F32))
    turn(1, 1)
    arrived(TSIB, ts.at[4], tr.at[4])
    cross_sum = factors(1, cross_sum)
    TOT[...] = exchange_end(TT2, TG2, as2, ar2, me_zc)

    valid = TOT[8:12] * (1.0 / 64.0)
    weight = valid * (512.0 / jnp.sum(valid))
    AL[0:4] = weight / TOT[0:4]
    BE[0:4] = weight / TOT[4:8]
    alpha = jnp.concatenate([AL[pl.ds(r, 1)] for r in my_rows], axis=1)
    beta = jnp.concatenate([BE[pl.ds(r, 1)] for r in my_rows], axis=1)
    for k in range(12):
        rr = slice(k * 128, (k + 1) * 128)
        grad = (ES[rr] * alpha - CP[rr] * beta).astype(BF16)
        GV[rr] = grad
        if k < 6:
            GTD[rr, my_half] = grad

    up, down, far = mod4(p + 1), mod4(p - 1), mod4(p + 2)

    def partial(n, p_):
        rows = []
        for i in range(4):
            rows.append(HDT[n, jnp.where(c == 0, i, p_), jnp.where(c == 0, p_, i)])
        return jnp.dot(jnp.concatenate(rows, axis=0), GV[...], preferred_element_type=F32)

    def put(ref, n, block):
        for i in range(4):
            ref[n, i] = block[i * CHIPCOL : (i + 1) * CHIPCOL].astype(ref.dtype)

    put(B1, 0, partial(0, far))
    send(B1.at[0], R1.at[0], q1s.at[0], q1r.at[0], at_p(up))
    put(B1, 1, partial(1, far))
    send(B1.at[1], R1.at[1], q1s.at[1], q1r.at[1], at_p(down))
    put(B1, 3, partial(0, down))
    send(B1.at[3], R1.at[3], q1s.at[3], q1r.at[3], at_p(down))
    put(B1, 2, partial(1, up))
    send(B1.at[2], R1.at[2], q1s.at[2], q1r.at[2], at_p(up))
    send(GV.at[VP : 2 * VP], GTD.at[:, my_half], gs.at[0], gr.at[0], sib)
    put(NEXT, 0, partial(0, up))
    put(NEXT, 1, partial(1, down))

    CR[...] = jnp.zeros_like(CR)
    for i in range(2):
        CR[pl.ds(my_rows[i], 1)] = cross_sum[:, i * 128 : (i + 1) * 128]
    exchange_start(CR, CG1, bs1, br1, me_xy, at_xy)

    def head_chunk(n):
        at = pl.ds(pl.multiple_of(n * 512, 512), 512)
        out = jnp.dot(GTD[...], H[:, at], preferred_element_type=F32)
        DH[:, at] = out[:SLAB].astype(BF16)

    def head_chunks(first, last):
        @pl.loop(first, last)
        def _(n):
            head_chunk(n)

    def relay(k):
        arrived(R1.at[k], q1s.at[k], q1r.at[k])
        near = up if k == 0 else down

        @pl.loop(0, 4)
        def _(i):
            F1[k, i] = (NEXT[k, i] + R1[k, i].astype(F32)).astype(BF16)

        send(F1.at[k], R1.at[4 + k], q1s.at[4 + k], q1r.at[4 + k], at_p(near))

    def second(k):
        arrived(R1.at[3 - k], q1s.at[3 - k], q1r.at[3 - k])
        arrived(R1.at[4 + k], q1s.at[4 + k], q1r.at[4 + k])

        @pl.loop(0, 4)
        def _(i):
            total = OWN[k, i] + R1[3 - k, i].astype(F32) + R1[4 + k, i].astype(F32)
            OWN[k, i] = total
            B2[k, i] = total.astype(BF16)

        for d in (2, 1, 3):
            n = k * 3 + d - 1
            to = mod4(q + d)
            send(B2.at[k, to], R2.at[k, d - 1], q2s.at[n], q2r.at[n], at_q(to))

    relay(0)
    put(OWN, 0, partial(0, p))
    put(OWN, 1, partial(1, p))
    relay(1)
    arrived(GTD.at[:, pl.ds(pl.multiple_of((1 - c) * HALF, HALF), HALF)], gs.at[0], gr.at[0])

    arrived(H.at[span(ROWS + (1 - c) * ROWS, ROWS)], cs.at[0], cr.at[0])

    @pl.when(c == 0)
    def _():
        arrived(H.at[3 * ROWS : 4 * ROWS], cs.at[1], cr.at[1])

    head_chunks(0, 2)
    head_chunks(2, 5)
    second(0)
    head_chunks(5, 6)
    second(1)
    CR2[...] = exchange_end(CR, CG1, bs1, br1, me_xy)
    exchange_start(CR2, CG2, bs2, br2, me_zc, at_zc)
    head_chunks(6, 7)

    at_home = (c == 0) & (zl == 0)
    at_home_hi = (c == 0) & (zl == 1)

    def to_owner(k, i, c_):
        n = k * 4 + i * 2 + c_
        return pltpu.make_async_remote_copy(
            src_ref=B3.at[k, i, c_], dst_ref=RZ.at[z], send_sem=rzs.at[n], recv_sem=rzr.at[z],
            device_id=dev(mod4(a + 2 * c + i), k, y, x, c_), device_id_type=MESH,
        )

    owners = [(k, i, c_) for k in range(2) for i in range(2) for c_ in range(2)]
    for k in range(2):
        total = OWN[k, q]
        for d in range(1, 4):
            arrived(R2.at[k, d - 1], q2s.at[k * 3 + d - 1], q2r.at[k * 3 + d - 1])
            total = total + R2[k, d - 1].astype(F32)
        for i in range(2):
            for c_ in range(2):
                B3[k, i, c_] = total[48 * c_ : 48 * c_ + 64, i * 128 : (i + 1) * 128].astype(BF16)
                if i == 0 and c_ == 0:
                    home = at_home if k == 0 else at_home_hi

                    @pl.when(jnp.logical_not(home))
                    def _():
                        to_owner(k, i, c_).start()

                    @pl.when(home)
                    def _():
                        RZ[z] = B3[k, 0, 0]
                else:
                    to_owner(k, i, c_).start()

    cross = exchange_end(CR2, CG2, bs2, br2, me_zc)
    KL[0:4] = cross[0:4] / TOT[4:8] - jnp.log(TOT[4:8]) + jnp.log(TOT[0:4])
    kl_out[...] = KL[pl.ds(a, 1)]

    for copy in pending:
        copy.wait_send()

    @pl.when(c == 1)
    def _():
        for make in later:
            make().wait_send()

    for k, i, c_ in owners:
        if i == 0 and c_ == 0:
            home = at_home if k == 0 else at_home_hi

            @pl.when(jnp.logical_not(home))
            def _():
                to_owner(k, i, c_).wait_send()
        else:
            to_owner(k, i, c_).wait_send()

    @pl.when(c == 1)
    def _():
        arrived(RZ.at[z], rzs.at[0], rzr.at[z])

    for k in range(1, 8):
        source = lax.rem(z + k, 8)
        arrived(RZ.at[source], rzs.at[0], rzr.at[source])
    total = RZ[0].astype(F32)
    for k in range(1, 8):
        total = total + RZ[k].astype(F32)
    dhid_out[...] = jnp.where(c == 0, total[0:56], total[8:64]).astype(BF16)


def on_device(hidden, valid_mask, student_head, teacher_logits):
    vm = pltpu.VMEM
    dma = pltpu.SemaphoreType.DMA
    any_spec = pl.BlockSpec(memory_space=pl.ANY)
    vmem_spec = pl.BlockSpec(memory_space=pltpu.VMEM)
    kl, dhid, dhead = pl.pallas_call(
        kernel,
        out_shape=(vm((1, ROWS), F32), vm((56, ROWS), BF16), vm((SLAB, D), BF16)),
        in_specs=[any_spec, vmem_spec, any_spec, any_spec],
        out_specs=(vmem_spec, vmem_spec, vmem_spec),
        scratch_shapes=[
            vm((512, D), BF16),
            vm((2 * VP, D), BF16),
            vm((2, 4, 4, CHIPCOL, 2 * VP), BF16),
            vm((256, 256), BF16),
            vm((3000, ROWS), BF16),
            vm((4, VP, ROWS), BF16),
            vm((4, VP, ROWS), BF16),
            vm((VP, ROWS), BF16),
            vm((2, VP, ROWS), BF16),
            vm((2 * VP, HALF), F32),
            vm((2 * VP, HALF), F32),
            vm((2 * VP, HALF), BF16),
            vm((VP, 512), BF16),
            vm((16, 128), F32),
            vm((16, 16, 128), F32),
            vm((16, 128), F32),
            vm((16, 16, 128), F32),
            vm((16, 128), F32),
            vm((8, 128), F32),
            vm((8, 128), F32),
            vm((8, 128), F32),
            vm((16, 8, 128), F32),
            vm((8, 128), F32),
            vm((16, 8, 128), F32),
            vm((8, 128), F32),
            vm((2, 4, CHIPCOL, HALF), F32),
            vm((2, 4, CHIPCOL, HALF), F32),
            vm((4, 4, CHIPCOL, HALF), BF16),
            vm((6, 4, CHIPCOL, HALF), BF16),
            vm((2, 4, CHIPCOL, HALF), BF16),
            vm((2, 4, CHIPCOL, HALF), BF16),
            vm((2, 3, CHIPCOL, HALF), BF16),
            vm((2, 2, 2, 64, 128), BF16),
            vm((8, 64, 128), BF16),
            dma((3,)),
            dma((3,)), dma((3,)),
            dma((2,)), dma((2,)),
            dma((2, 3)), dma((2, 3)), dma((2, 6)), dma((2, 6)),
            dma((2,)), dma((2,)),
            dma((5,)), dma((5,)),
            dma((1,)), dma((1,)),
            dma((15,)), dma((15,)), dma((15,)), dma((15,)),
            dma((15,)), dma((15,)), dma((15,)), dma((15,)),
            dma((6,)), dma((6,)), dma((6,)), dma((6,)),
            dma((8,)), dma((8,)),
        ],
        compiler_params=pltpu.CompilerParams(
            collective_id=0, has_side_effects=True, vmem_limit_bytes=50 * 1024 * 1024
        ),
        cost_estimate=pl.CostEstimate(flops=3 * 2 * 512 * 750 * 3584, bytes_accessed=13_000_000, transcendentals=0),
    )(hidden, valid_mask.reshape(1, ROWS), student_head, teacher_logits.T)
    return kl.reshape(ROWS), dhid.T, dhead


def solution(mesh):
    return jax.shard_map(
        on_device,
        mesh=mesh,
        in_specs=(P("tok", None), P("tok"), P(("voc", "tok"), None), P("tok", "voc")),
        out_specs=(P("tok"), P("tok", "voc"), P(("voc", "tok"), None)),
        check_vma=False,
    )
```

time: 519 us -> 74.7 us (0.14)
  waiting for transfers between devices: 353 us -> 0 us
  blocking collectives: 110 us -> 0 us
  Pallas kernels: 0 us -> 69.5 us
  matrix products: 24.4 us -> 0 us
  between operations: 14.5 us -> 0.64 us
  starting transfers between devices: 9.09 us -> 0 us
    reduce_scatter x2 -> x0, waiting for transfers between devices: 307 us -> none  [the longest x1 287 us: on_device(): lax.psum_scatter(partial_grad, 'voc', scatter_dimension=1, tiled=True)]
    psum x1 -> x0, blocking collectives: 81.4 us -> none  [on_device(): lax.psum((jnp.sum(student_exp, axis=1), jnp.sum(teacher_exp, axis=1), cro...]
    pallas_call x0 -> x1, Pallas kernels: none -> 69.5 us  [on_device(): pl.pallas_call(kernel, out_shape=(vm((1, ROWS), F32), vm((56, ROWS), BF16...]
    all_gather x1 -> x0, waiting for transfers between devices: 45.1 us -> none  [on_device(): lax.all_gather(hidden, 'tok', axis=0, tiled=True)]
    all_gather x1 -> x0, blocking collectives: 28.5 us -> none  [on_device(): lax.all_gather(valid_mask.astype(jnp.bfloat16), 'tok', axis=0, tiled=True)]
    dot_general x3 -> x0, matrix products: 24.4 us -> none  [the longest x1 9.24 us: on_device(): jnp.dot(grad, student_head, preferred_element_type=jnp.float32)]
    all_to_all x1 -> x0, starting transfers between devices: 9.01 us -> none  [on_device(): lax.all_to_all(teacher_logits, 'tok', split_axis=1, concat_axis=0, tiled=...]
  transfers between devices with their start and end apart: 4 -> 0, of which waited for: 3 -> 0; matrix products, arithmetic and copies ran while one was open for 2% -> 0% of each run, Pallas kernels for 0% -> 0%
where the time goes in v1:
time: 74.7 us; the launch traced here: 73.6 us
  Pallas kernels  69.5 us (93%)
  local copies, waits for them, and re-layouts  3.52 us (5%)
    pallas_call x1, Pallas kernels, on_device(): pl.pallas_call(kernel, out_shape=(vm((1, ROWS), F32), vm((56, ROWS), BF16...  69.5 us
    unnamed x3, local copies, waits for them, and re-layouts  3.52 us

profile of v1, /device:TPU:1, one launch (start us, length us, event | category | flops | bytes accessed | tf_op | source)
XLA Modules:
  0.0 73.6 jit_solution(11493619383854840895)
XLA Ops:
  0.6 69.5 %shard_map.67 = (f32[1,128]{1,0:T(1,128)S(1)}, bf16[56,128]{1,0:T(8,128)(2,1)S(1)}, bf16[750,3584]{1,0:T(8,128)(2,1)S(1)}) custom-call(bf16[128,3584]{1,0:T(8,128)(2,1)} %hid.1, s32[1,128]{1,0:T(1,128)} %bitcast.7, bf16[750,3584]{1,0:T(8,128)(2,1)} %head.1, bf16[3000,128]{1,0:T(8,128)(2,1)} %bitcast.6), custom_call_target="tpu_custom_call" | custom-call | flops 8257536000 | bytes 13000000 | tf_op jit(solution)/shard_map/pallas_call | solution.py:486
  70.1 0.5 copy.10
  70.6 0.6 copy.11
  71.2 2.4 %copy.12 = bf16[750,3584]{1,0:T(8,128)(2,1)} copy(bf16[750,3584]{1,0:T(8,128)(2,1)S(1)} %get-tuple-element.11) | data formatting | bytes 10752000

commit v2 on v1

--- a/solution.py
+++ b/solution.py
@@ -25,7 +25,7 @@
     TT, TG1, TT2, TG2, TOT, AL, BE, CR, CG1, CR2, CG2, KL,
     OWN, NEXT, B1, R1, F1, B2, R2, B3, RZ,
     local, hs, hr, zs, zr, p1s, p1r, p2s, p2r, cs, cr, ts, tr, gs, gr,
-    as1, ar1, as2, ar2, bs1, br1, bs2, br2, q1s, q1r, q2s, q2r, rzs, rzr,
+    as1, ar1, as2, ar2, bs1, br1, bs2, br2, q1s, q1r, f1s, f1r, q2s, q2r, rzs, rzr,
 ):
     a = lax.axis_index("tok")
     v = lax.axis_index("voc")
@@ -81,8 +81,6 @@
     load_teach.start()
     load_hid = pltpu.make_async_copy(hid, H.at[pl.ds(0, ROWS)], local.at[1])
     load_hid.start()
-    load_head = pltpu.make_async_copy(head, DH, local.at[2])
-    load_head.start()
 
     barrier = pltpu.get_barrier_semaphore()
     for k in range(1, 16):
@@ -125,6 +123,12 @@
         hid.at[span(p * PIECE, PIECE), cols(q)], H.at[span(base(g) + p * PIECE, PIECE), cols(q)],
         zs.at[g], zr.at[g], at_a(mod4(a - 1 - c - g)),
     )))
+
+    load_head = pltpu.make_async_copy(head.at[pl.ds(0, 736)], HD.at[0:736], local.at[2])
+    load_head.start()
+    send(head.at[pl.ds(0, 736)], HD.at[VP : VP + 736], hs.at[0], hr.at[0], sib)
+    load_tail = pltpu.make_async_copy(head, DH, local.at[3])
+    load_tail.start()
 
     load_teach.wait()
     place = lax.broadcasted_iota(jnp.int32, (VP, ROWS), 0)
@@ -143,8 +147,6 @@
         teacher_sum = teacher_sum + jnp.sum(jnp.exp(part), axis=0, keepdims=True)
     way = jnp.where(c == 0, 1, 3)
     send(TS.at[mod4(a + 2)], RLY, ts.at[2], tr.at[2], at_a(mod4(a + way)))
-    send(TS.at[mod4(a + 1)], TR.at[3], ts.at[0], tr.at[0], at_a(mod4(a + 1)))
-    send(TS.at[mod4(a + 3)], TR.at[1], ts.at[1], tr.at[1], at_a(mod4(a + 3)))
     TR[0] = TS[a]
 
     TT[...] = jnp.zeros_like(TT)
@@ -181,36 +183,43 @@
 
     each_group(first_step)
 
+    load_tail.wait()
+    HD[736:768] = jnp.concatenate([DH[736:750].astype(F32), jnp.zeros((18, D), F32)], axis=0).astype(BF16)
+    send(HD.at[736:768], HD.at[VP + 736 : VP + 768], hs.at[1], hr.at[1], sib)
     load_head.wait()
-    for k in range(3):
-        if k == 2:
-            HD[736:768] = jnp.concatenate([DH[736:750].astype(F32), jnp.zeros((18, D), F32)], axis=0).astype(BF16)
-
-        @pl.loop(k * 8, min(k * 8 + 8, 23))
-        def _(i):
-            HD[pl.ds(pl.multiple_of(i * 32, 32), 32)] = DH[pl.ds(pl.multiple_of(i * 32, 32), 32)]
-
-        send(HD.at[k * 256 : (k + 1) * 256], HD.at[VP + k * 256 : VP + (k + 1) * 256], hs.at[k], hr.at[k], sib)
 
     def first_end(g):
         for d in range(1, 4):
             arrived(piece(g, mod4(p - d)), p1s.at[g, d - 1], p1r.at[g, d - 1])
 
-    each_group(first_end)
-
     right, left = at_q(mod4(q + 1)), at_q(mod4(q - 1))
     before, after, across = mod4(q - 1), mod4(q + 1), mod4(q + 2)
 
     def part_of(g, half, q_):
         return H.at[span(base(g) + half * 64, 64), cols(q_)]
 
-    def pass_on(n, half, q_, to):
-        each_group(lambda g: send_group(g, lambda g: remote(
-            part_of(g, half, q_), part_of(g, half, q_), p2s.at[g, n], p2r.at[g, n], to,
-        )))
+    def pass_on(g, n, half, q_, to):
+        send_group(g, lambda g: remote(part_of(g, half, q_), part_of(g, half, q_), p2s.at[g, n], p2r.at[g, n], to))
 
     def passed(n, half, q_):
         each_group(lambda g: arrived(part_of(g, half, q_), p2s.at[g, n], p2r.at[g, n]))
+
+    def second_step(g):
+        first_end(g)
+        pass_on(g, 0, 0, q, right)
+        pass_on(g, 1, 1, q, left)
+        pass_on(g, 2, 1, q, right)
+        pass_on(g, 3, 0, q, left)
+
+    def relay_step(g):
+        arrived(part_of(g, 0, before), p2s.at[g, 0], p2r.at[g, 0])
+        pass_on(g, 4, 0, before, right)
+        arrived(part_of(g, 1, after), p2s.at[g, 1], p2r.at[g, 1])
+        pass_on(g, 5, 1, after, left)
+
+    each_group(second_step)
+    send(TS.at[mod4(a + 1)], TR.at[3], ts.at[0], tr.at[0], at_a(mod4(a + 1)))
+    send(TS.at[mod4(a + 3)], TR.at[1], ts.at[1], tr.at[1], at_a(mod4(a + 3)))
 
     my_half = pl.ds(pl.multiple_of(c * HALF, HALF), HALF)
 
@@ -219,51 +228,43 @@
         out = lax.dot_general(HD[rr, cols(q_)], H[my_half, cols(q_)], nt, preferred_element_type=F32)
         CP[rr] = out if first else CP[rr] + out
 
-    pass_on(0, 0, q, right)
-    pass_on(1, 1, q, left)
-    pass_on(2, 1, q, right)
-    pass_on(3, 0, q, left)
     load_hid.wait()
     logits(0, q, True)
     turn(0, 0)
-    passed(0, 0, before)
-    pass_on(4, 0, before, right)
-    passed(1, 1, after)
-    pass_on(5, 1, after, left)
+    each_group(relay_step)
+
+    arrived(RLY, ts.at[2], tr.at[2])
+    send(RLY, TR.at[2], ts.at[3], tr.at[3], at_a(mod4(a + way)))
     turn(0, 1)
     passed(2, 1, before)
     logits(0, before)
     passed(3, 0, after)
     logits(0, after)
-    for k in range(3):
-        arrived(HD.at[VP + k * 256 : VP + (k + 1) * 256], hs.at[k], hr.at[k])
+    arrived(HD.at[VP : VP + 736], hs.at[0], hr.at[0])
+    arrived(HD.at[VP + 736 : VP + 768], hs.at[1], hr.at[1])
     logits(1, q, True)
     logits(1, before)
     logits(1, after)
     passed(4, 0, across)
     passed(5, 1, across)
+    in_slab = lax.broadcasted_iota(jnp.int32, (256, HALF), 0) < SLAB - 512
+
+    def exponentials(slab, student_sum):
+        for k in range(3):
+            rr = slice(slab * VP + k * 256, slab * VP + (k + 1) * 256)
+            capped = CAP * jnp.tanh(CP[rr] * (1.0 / CAP))
+            exps = jnp.exp(capped)
+            if k == 2:
+                exps = jnp.where(in_slab, exps, 0.0)
+            CP[rr] = capped
+            ES[rr] = exps
+            student_sum = student_sum + jnp.sum(exps, axis=0, keepdims=True)
+        return student_sum
+
     logits(0, across)
     logits(1, across)
-
-    arrived(RLY, ts.at[2], tr.at[2])
-    send(RLY, TR.at[2], ts.at[3], tr.at[3], at_a(mod4(a + way)))
-
-    def share(g):
-        return H.at[span(base(g), ROWS)]
-
-    each_group(lambda g: send_group(g, lambda g: remote(share(g), share(g), cs.at[g], cr.at[g], sib)))
-
-    in_slab = lax.broadcasted_iota(jnp.int32, (256, HALF), 0) < SLAB - 512
-    student_sum = jnp.zeros((1, HALF), F32)
-    for k in range(6):
-        rr = slice(k * 256, (k + 1) * 256)
-        capped = CAP * jnp.tanh(CP[rr] * (1.0 / CAP))
-        exps = jnp.exp(capped)
-        if k % 3 == 2:
-            exps = jnp.where(in_slab, exps, 0.0)
-        CP[rr] = capped
-        ES[rr] = exps
-        student_sum = student_sum + jnp.sum(exps, axis=0, keepdims=True)
+    student_sum = exponentials(0, jnp.zeros((1, HALF), F32))
+    student_sum = exponentials(1, student_sum)
     my_rows = (mod4(a + 2 * c), mod4(a + 2 * c + 1))
     for i in range(2):
         TT[pl.ds(my_rows[i], 1)] = student_sum[:, i * 128 : (i + 1) * 128]
@@ -282,6 +283,11 @@
         return total
 
     exchange_start(TT, TG1, as1, ar1, me_xy, at_xy)
+
+    def share(g):
+        return H.at[span(base(g), ROWS)]
+
+    each_group(lambda g: send_group(g, lambda g: remote(share(g), share(g), cs.at[g], cr.at[g], sib)))
 
     def factors(slab, cross_sum):
         for k in range(6):
@@ -301,15 +307,21 @@
         return cross_sum
 
     turn(1, 0)
+
+    def give(i):
+        send(TR.at[2 * (1 - c) + i], TSIB.at[i], ts.at[4 + i], tr.at[4 + i], sib)
+
+    arrived(TR.at[3], ts.at[0], tr.at[0])
+    arrived(TR.at[1], ts.at[1], tr.at[1])
+    give(1)
     TT2[...] = exchange_end(TT, TG1, as1, ar1, me_xy)
     exchange_start(TT2, TG2, as2, ar2, me_zc, at_zc)
-    arrived(TR.at[3], ts.at[0], tr.at[0])
-    arrived(TR.at[1], ts.at[1], tr.at[1])
     arrived(TR.at[2], ts.at[3], tr.at[3])
-    send(TR.at[pl.ds(2 * (1 - c), 2)], TSIB, ts.at[4], tr.at[4], sib)
+    give(0)
     cross_sum = factors(0, jnp.zeros((1, HALF), F32))
     turn(1, 1)
-    arrived(TSIB, ts.at[4], tr.at[4])
+    for i in range(2):
+        arrived(TSIB.at[i], ts.at[4 + i], tr.at[4 + i])
     cross_sum = factors(1, cross_sum)
     TOT[...] = exchange_end(TT2, TG2, as2, ar2, me_zc)
 
@@ -365,37 +377,31 @@
         def _(n):
             head_chunk(n)
 
+    qup, qdown, qfar = mod4(q + 1), mod4(q - 1), mod4(q + 2)
+    order = (qfar, qup, qdown, q)
+
     def relay(k):
         arrived(R1.at[k], q1s.at[k], q1r.at[k])
         near = up if k == 0 else down
-
-        @pl.loop(0, 4)
-        def _(i):
+        for n, i in enumerate(order):
             F1[k, i] = (NEXT[k, i] + R1[k, i].astype(F32)).astype(BF16)
-
-        send(F1.at[k], R1.at[4 + k], q1s.at[4 + k], q1r.at[4 + k], at_p(near))
-
-    def second(k):
-        arrived(R1.at[3 - k], q1s.at[3 - k], q1r.at[3 - k])
-        arrived(R1.at[4 + k], q1s.at[4 + k], q1r.at[4 + k])
-
-        @pl.loop(0, 4)
-        def _(i):
-            total = OWN[k, i] + R1[3 - k, i].astype(F32) + R1[4 + k, i].astype(F32)
+            send(F1.at[k, i], R1.at[4 + k, i], f1s.at[k, n], f1r.at[k, n], at_p(near))
+
+    def second(k, n):
+        i = order[n]
+        arrived(R1.at[4 + k, i], f1s.at[k, n], f1r.at[k, n])
+        total = OWN[k, i] + R1[3 - k, i].astype(F32) + R1[4 + k, i].astype(F32)
+        if n == 3:
             OWN[k, i] = total
+        else:
             B2[k, i] = total.astype(BF16)
-
-        for d in (2, 1, 3):
-            n = k * 3 + d - 1
-            to = mod4(q + d)
-            send(B2.at[k, to], R2.at[k, d - 1], q2s.at[n], q2r.at[n], at_q(to))
+            send(B2.at[k, i], R2.at[k, n], q2s.at[k * 3 + n], q2r.at[k * 3 + n], at_q(i))
 
     relay(0)
+    relay(1)
     put(OWN, 0, partial(0, p))
     put(OWN, 1, partial(1, p))
-    relay(1)
     arrived(GTD.at[:, pl.ds(pl.multiple_of((1 - c) * HALF, HALF), HALF)], gs.at[0], gr.at[0])
-
     arrived(H.at[span(ROWS + (1 - c) * ROWS, ROWS)], cs.at[0], cr.at[0])
 
     @pl.when(c == 0)
@@ -403,13 +409,14 @@
         arrived(H.at[3 * ROWS : 4 * ROWS], cs.at[1], cr.at[1])
 
     head_chunks(0, 2)
-    head_chunks(2, 5)
-    second(0)
-    head_chunks(5, 6)
-    second(1)
+    arrived(R1.at[3], q1s.at[3], q1r.at[3])
+    arrived(R1.at[2], q1s.at[2], q1r.at[2])
+    for n in range(4):
+        for k in range(2):
+            second(k, n)
     CR2[...] = exchange_end(CR, CG1, bs1, br1, me_xy)
     exchange_start(CR2, CG2, bs2, br2, me_zc, at_zc)
-    head_chunks(6, 7)
+    head_chunks(2, 4)
 
     at_home = (c == 0) & (zl == 0)
     at_home_hi = (c == 0) & (zl == 1)
@@ -424,9 +431,9 @@
     owners = [(k, i, c_) for k in range(2) for i in range(2) for c_ in range(2)]
     for k in range(2):
         total = OWN[k, q]
-        for d in range(1, 4):
-            arrived(R2.at[k, d - 1], q2s.at[k * 3 + d - 1], q2r.at[k * 3 + d - 1])
-            total = total + R2[k, d - 1].astype(F32)
+        for n in range(3):
+            arrived(R2.at[k, n], q2s.at[k * 3 + n], q2r.at[k * 3 + n])
+            total = total + R2[k, n].astype(F32)
         for i in range(2):
             for c_ in range(2):
                 B3[k, i, c_] = total[48 * c_ : 48 * c_ + 64, i * 128 : (i + 1) * 128].astype(BF16)
@@ -443,6 +450,7 @@
                 else:
                     to_owner(k, i, c_).start()
 
+    head_chunks(4, 7)
     cross = exchange_end(CR2, CG2, bs2, br2, me_zc)
     KL[0:4] = cross[0:4] / TOT[4:8] - jnp.log(TOT[4:8]) + jnp.log(TOT[0:4])
     kl_out[...] = KL[pl.ds(a, 1)]
@@ -523,16 +531,16 @@
             vm((2, 3, CHIPCOL, HALF), BF16),
             vm((2, 2, 2, 64, 128), BF16),
             vm((8, 64, 128), BF16),
-            dma((3,)),
-            dma((3,)), dma((3,)),
+            dma((4,)),
+            dma((2,)), dma((2,)),
             dma((2,)), dma((2,)),
             dma((2, 3)), dma((2, 3)), dma((2, 6)), dma((2, 6)),
             dma((2,)), dma((2,)),
-            dma((5,)), dma((5,)),
+            dma((6,)), dma((6,)),
             dma((1,)), dma((1,)),
             dma((15,)), dma((15,)), dma((15,)), dma((15,)),
             dma((15,)), dma((15,)), dma((15,)), dma((15,)),
-            dma((6,)), dma((6,)), dma((6,)), dma((6,)),
+            dma((4,)), dma((4,)), dma((2, 4)), dma((2, 4)), dma((6,)), dma((6,)),
             dma((8,)), dma((8,)),
         ],
         compiler_params=pltpu.CompilerParams(

time: 74.7 us -> 72.6 us (0.972)
  Pallas kernels: 69.5 us -> 67.2 us
    pallas_call x1, Pallas kernels: 69.5 us -> 67.2 us  [on_device(): pl.pallas_call(kernel, out_shape=(vm((1, ROWS), F32), vm((56, ROWS), BF16...]
where the time goes in v2:
time: 72.6 us; the launch traced here: 71.4 us
  Pallas kernels  67.2 us (93%)
  local copies, waits for them, and re-layouts  3.52 us (5%)
    pallas_call x1, Pallas kernels, on_device(): pl.pallas_call(kernel, out_shape=(vm((1, ROWS), F32), vm((56, ROWS), BF16...  67.2 us
    unnamed x3, local copies, waits for them, and re-layouts  3.52 us

profile of v2, /device:TPU:1, one launch (start us, length us, event | category | flops | bytes accessed | tf_op | source)
XLA Modules:
  0.0 71.4 jit_solution(8786875554820169218)
XLA Ops:
  0.6 67.2 %shard_map.67 = (f32[1,128]{1,0:T(1,128)S(1)}, bf16[56,128]{1,0:T(8,128)(2,1)S(1)}, bf16[750,3584]{1,0:T(8,128)(2,1)S(1)}) custom-call(bf16[128,3584]{1,0:T(8,128)(2,1)} %hid.1, s32[1,128]{1,0:T(1,128)} %bitcast.7, bf16[750,3584]{1,0:T(8,128)(2,1)} %head.1, bf16[3000,128]{1,0:T(8,128)(2,1)} %bitcast.6), custom_call_target="tpu_custom_call" | custom-call | flops 8257536000 | bytes 13000000 | tf_op jit(solution)/shard_map/pallas_call | solution.py:494
  67.9 0.5 copy.10
  68.4 0.6 copy.11
  69.0 2.4 %copy.12 = bf16[750,3584]{1,0:T(8,128)(2,1)} copy(bf16[750,3584]{1,0:T(8,128)(2,1)S(1)} %get-tuple-element.11) | data formatting | bytes 10752000

commit v3 on v2

--- a/solution.py
+++ b/solution.py
@@ -77,15 +77,17 @@
             src_ref=dst, dst_ref=dst, send_sem=ssem, recv_sem=rsem, device_id=sib, device_id_type=MESH
         ).wait_recv()
 
+    barrier = pltpu.get_barrier_semaphore()
+    for k in range(1, 16):
+        pl.semaphore_signal(barrier, inc=1, device_id=at_zc(lax.rem(me_zc + k, 16)), device_id_type=MESH)
+    for k in range(1, 16):
+        pl.semaphore_signal(barrier, inc=1, device_id=at_xy(lax.rem(me_xy + k, 16)), device_id_type=MESH)
+
     load_teach = pltpu.make_async_copy(teach, tin, local.at[0])
     load_teach.start()
     load_hid = pltpu.make_async_copy(hid, H.at[pl.ds(0, ROWS)], local.at[1])
     load_hid.start()
 
-    barrier = pltpu.get_barrier_semaphore()
-    for k in range(1, 16):
-        pl.semaphore_signal(barrier, inc=1, device_id=at_xy(lax.rem(me_xy + k, 16)), device_id_type=MESH)
-        pl.semaphore_signal(barrier, inc=1, device_id=at_zc(lax.rem(me_zc + k, 16)), device_id_type=MESH)
     pl.semaphore_wait(barrier, 30)
 
     def span(start, size):
@@ -121,7 +123,8 @@
 
     each_group(lambda g: send_group(g, lambda g: remote(
         hid.at[span(p * PIECE, PIECE), cols(q)], H.at[span(base(g) + p * PIECE, PIECE), cols(q)],
-        zs.at[g], zr.at[g], at_a(mod4(a - 1 - c - g)),
+        zs.at[g], zr.at[g],
+        dev(mod4(a - 1 - c - g), jnp.where((c == 1) & (g == 0), 1 - zl, zl), y, x, c),
     )))
 
     load_head = pltpu.make_async_copy(head.at[pl.ds(0, 736)], HD.at[0:736], local.at[2])
@@ -187,6 +190,7 @@
     HD[736:768] = jnp.concatenate([DH[736:750].astype(F32), jnp.zeros((18, D), F32)], axis=0).astype(BF16)
     send(HD.at[736:768], HD.at[VP + 736 : VP + 768], hs.at[1], hr.at[1], sib)
     load_head.wait()
+    turn(0, 0)
 
     def first_end(g):
         for d in range(1, 4):
@@ -230,12 +234,11 @@
 
     load_hid.wait()
     logits(0, q, True)
-    turn(0, 0)
+    turn(0, 1)
     each_group(relay_step)
 
     arrived(RLY, ts.at[2], tr.at[2])
     send(RLY, TR.at[2], ts.at[3], tr.at[3], at_a(mod4(a + way)))
-    turn(0, 1)
     passed(2, 1, before)
     logits(0, before)
     passed(3, 0, after)
@@ -283,11 +286,6 @@
         return total
 
     exchange_start(TT, TG1, as1, ar1, me_xy, at_xy)
-
-    def share(g):
-        return H.at[span(base(g), ROWS)]
-
-    each_group(lambda g: send_group(g, lambda g: remote(share(g), share(g), cs.at[g], cr.at[g], sib)))
 
     def factors(slab, cross_sum):
         for k in range(6):
@@ -359,13 +357,12 @@
     put(B1, 2, partial(1, up))
     send(B1.at[2], R1.at[2], q1s.at[2], q1r.at[2], at_p(up))
     send(GV.at[VP : 2 * VP], GTD.at[:, my_half], gs.at[0], gr.at[0], sib)
-    put(NEXT, 0, partial(0, up))
-    put(NEXT, 1, partial(1, down))
-
-    CR[...] = jnp.zeros_like(CR)
-    for i in range(2):
-        CR[pl.ds(my_rows[i], 1)] = cross_sum[:, i * 128 : (i + 1) * 128]
-    exchange_start(CR, CG1, bs1, br1, me_xy, at_xy)
+
+    def share(g):
+        return H.at[span(base(g), ROWS)]
+
+    each_group(lambda g: send_group(g, lambda g: remote(share(g), share(g), cs.at[g], cr.at[g], sib)))
+
 
     def head_chunk(n):
         at = pl.ds(pl.multiple_of(n * 512, 512), 512)
@@ -397,8 +394,16 @@
             B2[k, i] = total.astype(BF16)
             send(B2.at[k, i], R2.at[k, n], q2s.at[k * 3 + n], q2r.at[k * 3 + n], at_q(i))
 
+    put(NEXT, 0, partial(0, up))
     relay(0)
+    put(NEXT, 1, partial(1, down))
     relay(1)
+
+    CR[...] = jnp.zeros_like(CR)
+    for i in range(2):
+        CR[pl.ds(my_rows[i], 1)] = cross_sum[:, i * 128 : (i + 1) * 128]
+    exchange_start(CR, CG1, bs1, br1, me_xy, at_xy)
+
     put(OWN, 0, partial(0, p))
     put(OWN, 1, partial(1, p))
     arrived(GTD.at[:, pl.ds(pl.multiple_of((1 - c) * HALF, HALF), HALF)], gs.at[0], gr.at[0])
@@ -408,7 +413,7 @@
     def _():
         arrived(H.at[3 * ROWS : 4 * ROWS], cs.at[1], cr.at[1])
 
-    head_chunks(0, 2)
+    head_chunks(0, 1)
     arrived(R1.at[3], q1s.at[3], q1r.at[3])
     arrived(R1.at[2], q1s.at[2], q1r.at[2])
     for n in range(4):
@@ -416,7 +421,7 @@
             second(k, n)
     CR2[...] = exchange_end(CR, CG1, bs1, br1, me_xy)
     exchange_start(CR2, CG2, bs2, br2, me_zc, at_zc)
-    head_chunks(2, 4)
+    head_chunks(1, 3)
 
     at_home = (c == 0) & (zl == 0)
     at_home_hi = (c == 0) & (zl == 1)
@@ -450,7 +455,7 @@
                 else:
                     to_owner(k, i, c_).start()
 
-    head_chunks(4, 7)
+    head_chunks(3, 7)
     cross = exchange_end(CR2, CG2, bs2, br2, me_zc)
     KL[0:4] = cross[0:4] / TOT[4:8] - jnp.log(TOT[4:8]) + jnp.log(TOT[0:4])
     kl_out[...] = KL[pl.ds(a, 1)]
@@ -484,6 +489,20 @@
     for k in range(1, 8):
         total = total + RZ[k].astype(F32)
     dhid_out[...] = jnp.where(c == 0, total[0:56], total[8:64]).astype(BF16)
+
+
+def results(kl, dhid, dhead, kl_out, dhid_out, dhead_out, sem):
+    copies = [
+        pltpu.make_async_copy(dhid, dhid_out, sem.at[7]),
+        pltpu.make_async_copy(kl, kl_out, sem.at[8]),
+    ]
+    for n in range(7):
+        at = pl.ds(n * 512, 512)
+        copies.append(pltpu.make_async_copy(dhead.at[:, at], dhead_out.at[:, at], sem.at[n]))
+    for copy in copies:
+        copy.start()
+    for copy in copies:
+        copy.wait()
 
 
 def on_device(hidden, valid_mask, student_head, teacher_logits):
@@ -548,6 +567,18 @@
         ),
         cost_estimate=pl.CostEstimate(flops=3 * 2 * 512 * 750 * 3584, bytes_accessed=13_000_000, transcendentals=0),
     )(hidden, valid_mask.reshape(1, ROWS), student_head, teacher_logits.T)
+    kl, dhid, dhead = pl.pallas_call(
+        results,
+        out_shape=(
+            jax.ShapeDtypeStruct((1, ROWS), F32),
+            jax.ShapeDtypeStruct((56, ROWS), BF16),
+            jax.ShapeDtypeStruct((SLAB, D), BF16),
+        ),
+        in_specs=[any_spec] * 3,
+        out_specs=(any_spec,) * 3,
+        scratch_shapes=[dma((9,))],
+        compiler_params=pltpu.CompilerParams(vmem_limit_bytes=1024 * 1024),
+    )(kl, dhid, dhead)
     return kl.reshape(ROWS), dhid.T, dhead
 
 

time: 72.6 us -> 71.3 us (0.982); the launches traced: 71.4 us -> 70.9 us
  local copies, waits for them, and re-layouts: 3.52 us -> 0 us
  Pallas kernels: 67.2 us -> 70.3 us
    unnamed x3 -> x0, local copies, waits for them, and re-layouts: 3.52 us -> none
    pallas_call x0 -> x1, Pallas kernels: none -> 2.48 us  [on_device(): pl.pallas_call(results, out_shape=(jax.ShapeDtypeStruct((1, ROWS), F32),...]
where the time goes in v3:
time: 71.3 us; the launch traced here: 70.9 us
  Pallas kernels  70.3 us (99%)
    pallas_call x1, Pallas kernels, on_device(): pl.pallas_call(kernel, out_shape=(vm((1, ROWS), F32), vm((56, ROWS), BF16...  67.8 us
    pallas_call x1, Pallas kernels, on_device(): pl.pallas_call(results, out_shape=(jax.ShapeDtypeStruct((1, ROWS), F32),...  2.48 us

profile of v3, /device:TPU:1, one launch (start us, length us, event | category | flops | bytes accessed | tf_op | source)
XLA Modules:
  0.0 70.9 jit_solution(13442316769040489640)
XLA Ops:
  0.6 67.8 %shard_map.67 = (f32[1,128]{1,0:T(1,128)S(1)}, bf16[56,128]{1,0:T(8,128)(2,1)S(1)}, bf16[750,3584]{1,0:T(8,128)(2,1)S(1)}) custom-call(bf16[128,3584]{1,0:T(8,128)(2,1)} %hid.1, s32[1,128]{1,0:T(1,128)} %bitcast.6, bf16[750,3584]{1,0:T(8,128)(2,1)} %head.1, bf16[3000,128]{1,0:T(8,128)(2,1)} %bitcast.4), custom_call_target="tpu_custom_call" | custom-call | flops 8257536000 | bytes 13000000 | tf_op jit(solution)/shard_map/pallas_call | solution.py:513
  68.5 2.5 %shard_map.68 = (f32[1,128]{1,0:T(1,128)}, bf16[56,128]{1,0:T(8,128)(2,1)}, bf16[750,3584]{1,0:T(8,128)(2,1)}) custom-call(f32[1,128]{1,0:T(1,128)S(1)} %get-tuple-element.9.kl, bf16[56,128]{1,0:T(8,128)(2,1)S(1)} %get-tuple-element.10.dhid, bf16[750,3584]{1,0:T(8,128)(2,1)S(1)} %get-tuple-element.11.dhead), custom_call_target="tpu_custom_call" | custom-call | tf_op jit(solution)/shard_map/pallas_call | solution.py:570

commit v4 on v3

--- a/solution.py
+++ b/solution.py
@@ -134,23 +134,21 @@
     load_tail.start()
 
     load_teach.wait()
-    place = lax.broadcasted_iota(jnp.int32, (VP, ROWS), 0)
-    teacher_sum = jnp.zeros((1, ROWS), F32)
     for t in range(4):
         start = t * SLAB // 16 * 16
-        off = t * SLAB - start
-        height = min(VP + 16, 3000 - start)
-        tall = tin[start : start + height].astype(F32)
-        if height < VP + 16:
-            tall = jnp.concatenate([tall, jnp.zeros((VP + 16 - height, ROWS), F32)], axis=0)
-        if off:
-            tall = pltpu.roll(tall, VP + 16 - off, 0)
-        part = jnp.where(place < SLAB, tall[:VP], -30000.0)
-        TS[t] = part.astype(BF16)
-        teacher_sum = teacher_sum + jnp.sum(jnp.exp(part), axis=0, keepdims=True)
+        if t < 3:
+            TS[t] = tin[start : start + VP]
+        else:
+            TS[t, 0 : VP - 16] = tin[start : start + VP - 16]
+            rest = tin[start + VP - 16 : 3000].astype(F32)
+            TS[t, VP - 16 : VP] = jnp.concatenate([rest, jnp.zeros((8, ROWS), F32)], axis=0).astype(BF16)
     way = jnp.where(c == 0, 1, 3)
     send(TS.at[mod4(a + 2)], RLY, ts.at[2], tr.at[2], at_a(mod4(a + way)))
     TR[0] = TS[a]
+    teacher_sum = jnp.zeros((1, ROWS), F32)
+    for start in range(0, 3000, 752):
+        part = tin[start : min(start + 752, 3000)].astype(F32)
+        teacher_sum = teacher_sum + jnp.sum(jnp.exp(part), axis=0, keepdims=True)
 
     TT[...] = jnp.zeros_like(TT)
     TT[pl.ds(4 + a, 1)] = teacher_sum
@@ -287,82 +285,87 @@
 
     exchange_start(TT, TG1, as1, ar1, me_xy, at_xy)
 
-    def factors(slab, cross_sum):
-        for k in range(6):
-            rr = slice(slab * VP + k * 128, slab * VP + (k + 1) * 128)
-            vv = slice(k * 128, (k + 1) * 128)
-            if slab == 0:
-                target = jnp.concatenate([TR[2 * c, vv], TR[2 * c + 1, vv]], axis=1).astype(F32)
-            else:
-                target = jnp.concatenate([TSIB[0, vv], TSIB[1, vv]], axis=1).astype(F32)
-            expd = jnp.exp(target)
-            capped = CP[rr]
-            cross_sum = cross_sum + jnp.sum(expd * (target - capped), axis=0, keepdims=True)
-            ratio = capped * (1.0 / CAP)
-            slope = 1.0 - ratio * ratio
-            ES[rr] = ES[rr] * slope
-            CP[rr] = expd * slope
-        return cross_sum
+    blocks = (3 * c, 1 + c)
+    toks = (mod4(a + 3 * c), mod4(a + 1 + c))
+    lanes = tuple(pl.ds(pl.multiple_of(n * 128, 128), 128) for n in (c, 1 - c))
+    shift = jnp.where(a == 0, 0, VP - 16 + 2 * a)
+    place = lax.broadcasted_iota(jnp.int32, (VP, ROWS), 0)
+
+    def give(k):
+        send(TR.at[(3 * (1 - c), 2 - c)[k]], TSIB.at[k], ts.at[4 + k], tr.at[4 + k], sib)
+
+    def align(tile):
+        tall = pltpu.roll(tile.astype(F32), shift, 0)
+        return jnp.where(place < SLAB, tall, -30000.0)
+
+    def factors(k, slab):
+        target = align(TR[blocks[k]] if slab == 0 else TSIB[k])
+        rr = slice(slab * VP, (slab + 1) * VP)
+        expd = jnp.exp(target)
+        capped = CP[rr, lanes[k]]
+        ratio = capped * (1.0 / CAP)
+        slope = 1.0 - ratio * ratio
+        ES[rr, lanes[k]] = ES[rr, lanes[k]] * slope
+        CP[rr, lanes[k]] = expd * slope
+        return jnp.sum(expd * (target - capped), axis=0, keepdims=True)
 
     turn(1, 0)
-
-    def give(i):
-        send(TR.at[2 * (1 - c) + i], TSIB.at[i], ts.at[4 + i], tr.at[4 + i], sib)
-
     arrived(TR.at[3], ts.at[0], tr.at[0])
-    arrived(TR.at[1], ts.at[1], tr.at[1])
-    give(1)
+    give(0)
+    cross_first = factors(0, 0)
     TT2[...] = exchange_end(TT, TG1, as1, ar1, me_xy)
     exchange_start(TT2, TG2, as2, ar2, me_zc, at_zc)
-    arrived(TR.at[2], ts.at[3], tr.at[3])
-    give(0)
-    cross_sum = factors(0, jnp.zeros((1, HALF), F32))
+    arrived(TSIB.at[0], ts.at[4], tr.at[4])
+    cross_first = cross_first + factors(0, 1)
     turn(1, 1)
-    for i in range(2):
-        arrived(TSIB.at[i], ts.at[4 + i], tr.at[4 + i])
-    cross_sum = factors(1, cross_sum)
     TOT[...] = exchange_end(TT2, TG2, as2, ar2, me_zc)
 
     valid = TOT[8:12] * (1.0 / 64.0)
     weight = valid * (512.0 / jnp.sum(valid))
     AL[0:4] = weight / TOT[0:4]
     BE[0:4] = weight / TOT[4:8]
-    alpha = jnp.concatenate([AL[pl.ds(r, 1)] for r in my_rows], axis=1)
-    beta = jnp.concatenate([BE[pl.ds(r, 1)] for r in my_rows], axis=1)
-    for k in range(12):
-        rr = slice(k * 128, (k + 1) * 128)
-        grad = (ES[rr] * alpha - CP[rr] * beta).astype(BF16)
-        GV[rr] = grad
-        if k < 6:
-            GTD[rr, my_half] = grad
-
-    up, down, far = mod4(p + 1), mod4(p - 1), mod4(p + 2)
-
-    def partial(n, p_):
+
+    def gradient(k):
+        alpha, beta = AL[pl.ds(toks[k], 1)], BE[pl.ds(toks[k], 1)]
+        at = pl.ds(pl.multiple_of(c * HALF + (c, 1 - c)[k] * 128, 128), 128)
+        for n in range(6):
+            rr = slice(n * 256, (n + 1) * 256)
+            grad = (ES[rr, lanes[k]] * alpha - CP[rr, lanes[k]] * beta).astype(BF16)
+            GV[rr, lanes[k]] = grad
+            if n < 3:
+                GTD[rr, at] = grad
+
+    def partial(k, p_):
         rows = []
         for i in range(4):
-            rows.append(HDT[n, jnp.where(c == 0, i, p_), jnp.where(c == 0, p_, i)])
-        return jnp.dot(jnp.concatenate(rows, axis=0), GV[...], preferred_element_type=F32)
+            for zl_ in range(2):
+                rows.append(HDT[zl_, jnp.where(c == 0, i, p_), jnp.where(c == 0, p_, i)])
+        return jnp.dot(jnp.concatenate(rows, axis=0), GV[:, lanes[k]], preferred_element_type=F32)
 
     def put(ref, n, block):
         for i in range(4):
-            ref[n, i] = block[i * CHIPCOL : (i + 1) * CHIPCOL].astype(ref.dtype)
-
+            for zl_ in range(2):
+                first = (i * 2 + zl_) * CHIPCOL
+                ref[n, i, zl_] = block[first : first + CHIPCOL].astype(ref.dtype)
+
+    up, down, far = mod4(p + 1), mod4(p - 1), mod4(p + 2)
+    gradient(0)
     put(B1, 0, partial(0, far))
     send(B1.at[0], R1.at[0], q1s.at[0], q1r.at[0], at_p(up))
+    put(B1, 3, partial(0, down))
+    send(B1.at[3], R1.at[3], q1s.at[3], q1r.at[3], at_p(down))
+    arrived(TR.at[1], ts.at[1], tr.at[1])
+    arrived(TR.at[2], ts.at[3], tr.at[3])
+    give(1)
+    put(NEXT, 0, partial(0, up))
+    cross_second = factors(1, 0)
+    arrived(TSIB.at[1], ts.at[5], tr.at[5])
+    cross_second = cross_second + factors(1, 1)
+    gradient(1)
     put(B1, 1, partial(1, far))
     send(B1.at[1], R1.at[1], q1s.at[1], q1r.at[1], at_p(down))
-    put(B1, 3, partial(0, down))
-    send(B1.at[3], R1.at[3], q1s.at[3], q1r.at[3], at_p(down))
     put(B1, 2, partial(1, up))
     send(B1.at[2], R1.at[2], q1s.at[2], q1r.at[2], at_p(up))
-    send(GV.at[VP : 2 * VP], GTD.at[:, my_half], gs.at[0], gr.at[0], sib)
-
-    def share(g):
-        return H.at[span(base(g), ROWS)]
-
-    each_group(lambda g: send_group(g, lambda g: remote(share(g), share(g), cs.at[g], cr.at[g], sib)))
-
 
     def head_chunk(n):
         at = pl.ds(pl.multiple_of(n * 512, 512), 512)
@@ -394,26 +397,23 @@
             B2[k, i] = total.astype(BF16)
             send(B2.at[k, i], R2.at[k, n], q2s.at[k * 3 + n], q2r.at[k * 3 + n], at_q(i))
 
-    put(NEXT, 0, partial(0, up))
     relay(0)
     put(NEXT, 1, partial(1, down))
     relay(1)
+    send(GV.at[VP : 2 * VP], GTD.at[:, my_half], gs.at[0], gr.at[0], sib)
+
+    def share(g):
+        return H.at[span(base(g), ROWS)]
+
+    each_group(lambda g: send_group(g, lambda g: remote(share(g), share(g), cs.at[g], cr.at[g], sib)))
 
     CR[...] = jnp.zeros_like(CR)
-    for i in range(2):
-        CR[pl.ds(my_rows[i], 1)] = cross_sum[:, i * 128 : (i + 1) * 128]
+    CR[pl.ds(toks[0], 1)] = cross_first
+    CR[pl.ds(toks[1], 1)] = cross_second
     exchange_start(CR, CG1, bs1, br1, me_xy, at_xy)
 
     put(OWN, 0, partial(0, p))
     put(OWN, 1, partial(1, p))
-    arrived(GTD.at[:, pl.ds(pl.multiple_of((1 - c) * HALF, HALF), HALF)], gs.at[0], gr.at[0])
-    arrived(H.at[span(ROWS + (1 - c) * ROWS, ROWS)], cs.at[0], cr.at[0])
-
-    @pl.when(c == 0)
-    def _():
-        arrived(H.at[3 * ROWS : 4 * ROWS], cs.at[1], cr.at[1])
-
-    head_chunks(0, 1)
     arrived(R1.at[3], q1s.at[3], q1r.at[3])
     arrived(R1.at[2], q1s.at[2], q1r.at[2])
     for n in range(4):
@@ -421,39 +421,43 @@
             second(k, n)
     CR2[...] = exchange_end(CR, CG1, bs1, br1, me_xy)
     exchange_start(CR2, CG2, bs2, br2, me_zc, at_zc)
-    head_chunks(1, 3)
-
-    at_home = (c == 0) & (zl == 0)
-    at_home_hi = (c == 0) & (zl == 1)
-
-    def to_owner(k, i, c_):
-        n = k * 4 + i * 2 + c_
+    arrived(GTD.at[:, pl.ds(pl.multiple_of((1 - c) * HALF, HALF), HALF)], gs.at[0], gr.at[0])
+    arrived(H.at[span(ROWS + (1 - c) * ROWS, ROWS)], cs.at[0], cr.at[0])
+
+    @pl.when(c == 0)
+    def _():
+        arrived(H.at[3 * ROWS : 4 * ROWS], cs.at[1], cr.at[1])
+
+    head_chunks(0, 3)
+
+    def to_owner(k, zl_, c_):
+        n = k * 4 + zl_ * 2 + c_
         return pltpu.make_async_remote_copy(
-            src_ref=B3.at[k, i, c_], dst_ref=RZ.at[z], send_sem=rzs.at[n], recv_sem=rzr.at[z],
-            device_id=dev(mod4(a + 2 * c + i), k, y, x, c_), device_id_type=MESH,
+            src_ref=B3.at[k, zl_, c_], dst_ref=RZ.at[z], send_sem=rzs.at[n], recv_sem=rzr.at[z],
+            device_id=dev(toks[k], zl_, y, x, c_), device_id_type=MESH,
         )
 
-    owners = [(k, i, c_) for k in range(2) for i in range(2) for c_ in range(2)]
+    owners = [(k, zl_, c_) for k in range(2) for zl_ in range(2) for c_ in range(2)]
     for k in range(2):
         total = OWN[k, q]
         for n in range(3):
             arrived(R2.at[k, n], q2s.at[k * 3 + n], q2r.at[k * 3 + n])
             total = total + R2[k, n].astype(F32)
-        for i in range(2):
+        for zl_ in range(2):
             for c_ in range(2):
-                B3[k, i, c_] = total[48 * c_ : 48 * c_ + 64, i * 128 : (i + 1) * 128].astype(BF16)
-                if i == 0 and c_ == 0:
-                    home = at_home if k == 0 else at_home_hi
+                B3[k, zl_, c_] = total[zl_, 48 * c_ : 48 * c_ + 64].astype(BF16)
+                if k == 0 and c_ == 0:
+                    home = (c == 0) & (zl == zl_)
 
                     @pl.when(jnp.logical_not(home))
                     def _():
-                        to_owner(k, i, c_).start()
+                        to_owner(k, zl_, c_).start()
 
                     @pl.when(home)
                     def _():
-                        RZ[z] = B3[k, 0, 0]
+                        RZ[z] = B3[k, zl_, c_]
                 else:
-                    to_owner(k, i, c_).start()
+                    to_owner(k, zl_, c_).start()
 
     head_chunks(3, 7)
     cross = exchange_end(CR2, CG2, bs2, br2, me_zc)
@@ -468,15 +472,14 @@
         for make in later:
             make().wait_send()
 
-    for k, i, c_ in owners:
-        if i == 0 and c_ == 0:
-            home = at_home if k == 0 else at_home_hi
-
-            @pl.when(jnp.logical_not(home))
+    for k, zl_, c_ in owners:
+        if k == 0 and c_ == 0:
+
+            @pl.when(jnp.logical_not((c == 0) & (zl == zl_)))
             def _():
-                to_owner(k, i, c_).wait_send()
+                to_owner(k, zl_, c_).wait_send()
         else:
-            to_owner(k, i, c_).wait_send()
+            to_owner(k, zl_, c_).wait_send()
 
     @pl.when(c == 1)
     def _():
@@ -541,13 +544,13 @@
             vm((8, 128), F32),
             vm((16, 8, 128), F32),
             vm((8, 128), F32),
-            vm((2, 4, CHIPCOL, HALF), F32),
-            vm((2, 4, CHIPCOL, HALF), F32),
-            vm((4, 4, CHIPCOL, HALF), BF16),
-            vm((6, 4, CHIPCOL, HALF), BF16),
-            vm((2, 4, CHIPCOL, HALF), BF16),
-            vm((2, 4, CHIPCOL, HALF), BF16),
-            vm((2, 3, CHIPCOL, HALF), BF16),
+            vm((2, 4, 2, CHIPCOL, 128), F32),
+            vm((2, 4, 2, CHIPCOL, 128), F32),
+            vm((4, 4, 2, CHIPCOL, 128), BF16),
+            vm((6, 4, 2, CHIPCOL, 128), BF16),
+            vm((2, 4, 2, CHIPCOL, 128), BF16),
+            vm((2, 4, 2, CHIPCOL, 128), BF16),
+            vm((2, 3, 2, CHIPCOL, 128), BF16),
             vm((2, 2, 2, 64, 128), BF16),
             vm((8, 64, 128), BF16),
             dma((4,)),

time: 71.3 us -> 77.8 us (1.091)
  Pallas kernels: 70.3 us -> 76.9 us
    pallas_call x1, Pallas kernels: 67.8 us -> 74.4 us  [on_device(): pl.pallas_call(kernel, out_shape=(vm((1, ROWS), F32), vm((56, ROWS), BF16...]
where the time goes in v4:
time: 77.8 us; the launch traced here: 77.7 us
  Pallas kernels  76.9 us (99%)
  between operations  0.8 us (1%)
    pallas_call x1, Pallas kernels, on_device(): pl.pallas_call(kernel, out_shape=(vm((1, ROWS), F32), vm((56, ROWS), BF16...  74.4 us
    pallas_call x1, Pallas kernels, on_device(): pl.pallas_call(results, out_shape=(jax.ShapeDtypeStruct((1, ROWS), F32),...  2.48 us

profile of v4, /device:TPU:1, one launch (start us, length us, event | category | flops | bytes accessed | tf_op | source)
XLA Modules:
  0.0 77.7 jit_solution(754997921172099942)
XLA Ops:
  0.6 74.4 %shard_map.67 = (f32[1,128]{1,0:T(1,128)S(1)}, bf16[56,128]{1,0:T(8,128)(2,1)S(1)}, bf16[750,3584]{1,0:T(8,128)(2,1)S(1)}) custom-call(bf16[128,3584]{1,0:T(8,128)(2,1)} %hid.1, s32[1,128]{1,0:T(1,128)} %bitcast.6, bf16[750,3584]{1,0:T(8,128)(2,1)} %head.1, bf16[3000,128]{1,0:T(8,128)(2,1)} %bitcast.4), custom_call_target="tpu_custom_call" | custom-call | flops 8257536000 | bytes 13000000 | tf_op jit(solution)/shard_map/pallas_call | solution.py:516
  75.0 2.5 %shard_map.68 = (f32[1,128]{1,0:T(1,128)}, bf16[56,128]{1,0:T(8,128)(2,1)}, bf16[750,3584]{1,0:T(8,128)(2,1)}) custom-call(f32[1,128]{1,0:T(1,128)S(1)} %get-tuple-element.9.kl, bf16[56,128]{1,0:T(8,128)(2,1)S(1)} %get-tuple-element.10.dhid, bf16[750,3584]{1,0:T(8,128)(2,1)S(1)} %get-tuple-element.11.dhead), custom_call_target="tpu_custom_call" | custom-call | tf_op jit(solution)/shard_map/pallas_call | solution.py:573

commit v5 on v3

--- a/solution.py
+++ b/solution.py
@@ -14,6 +14,7 @@
 QCOL = D // 4
 PIECE = ROWS // 4
 CHIPCOL = 112
+FAR_FIRST = (8, 10, 6, 9, 7, 11, 5, 12, 4, 2, 14, 13, 3, 15, 1)
 MESH = pl.DeviceIdType.MESH
 F32 = jnp.float32
 BF16 = jnp.bfloat16
@@ -78,7 +79,7 @@
         ).wait_recv()
 
     barrier = pltpu.get_barrier_semaphore()
-    for k in range(1, 16):
+    for k in FAR_FIRST:
         pl.semaphore_signal(barrier, inc=1, device_id=at_zc(lax.rem(me_zc + k, 16)), device_id_type=MESH)
     for k in range(1, 16):
         pl.semaphore_signal(barrier, inc=1, device_id=at_xy(lax.rem(me_xy + k, 16)), device_id_type=MESH)
@@ -100,6 +101,18 @@
         return ROWS + c * ROWS + g * ROWS
 
     later = []
+
+    def flush():
+        for copy in pending:
+            copy.wait_send()
+        pending.clear()
+
+        @pl.when(c == 1)
+        def _():
+            for make in later:
+                make().wait_send()
+
+        later.clear()
 
     def each_group(step):
         step(0)
@@ -135,7 +148,6 @@
 
     load_teach.wait()
     place = lax.broadcasted_iota(jnp.int32, (VP, ROWS), 0)
-    teacher_sum = jnp.zeros((1, ROWS), F32)
     for t in range(4):
         start = t * SLAB // 16 * 16
         off = t * SLAB - start
@@ -147,14 +159,9 @@
             tall = pltpu.roll(tall, VP + 16 - off, 0)
         part = jnp.where(place < SLAB, tall[:VP], -30000.0)
         TS[t] = part.astype(BF16)
-        teacher_sum = teacher_sum + jnp.sum(jnp.exp(part), axis=0, keepdims=True)
     way = jnp.where(c == 0, 1, 3)
     send(TS.at[mod4(a + 2)], RLY, ts.at[2], tr.at[2], at_a(mod4(a + way)))
     TR[0] = TS[a]
-
-    TT[...] = jnp.zeros_like(TT)
-    TT[pl.ds(4 + a, 1)] = teacher_sum
-    TT[pl.ds(8 + a, 1)] = mask[...].astype(F32)
 
     nt = (((1,), (1,)), ((), ()))
     EYE[...] = jnp.where(
@@ -179,12 +186,19 @@
 
     def first_step(g):
         arrived(piece(g, p), zs.at[g], zr.at[g])
-        for d in range(1, 4):
+        for d in (2, 1, 3):
             send_group(g, lambda g, d=d: remote(
                 piece(g, p), piece(g, p), p1s.at[g, d - 1], p1r.at[g, d - 1], at_p(mod4(p + d)),
             ))
 
     each_group(first_step)
+
+    TT[...] = jnp.zeros_like(TT)
+    teacher_sum = jnp.zeros((1, ROWS), F32)
+    for t in range(4):
+        teacher_sum = teacher_sum + jnp.sum(jnp.exp(TS[t].astype(F32)), axis=0, keepdims=True)
+    TT[pl.ds(4 + a, 1)] = teacher_sum
+    TT[pl.ds(8 + a, 1)] = mask[...].astype(F32)
 
     load_tail.wait()
     HD[736:768] = jnp.concatenate([DH[736:750].astype(F32), jnp.zeros((18, D), F32)], axis=0).astype(BF16)
@@ -273,7 +287,7 @@
         TT[pl.ds(my_rows[i], 1)] = student_sum[:, i * 128 : (i + 1) * 128]
 
     def exchange_start(tile, slots, ssem, rsem, me, at):
-        for k in range(1, 16):
+        for k in FAR_FIRST:
             send(tile, slots.at[me], ssem.at[k - 1], rsem.at[k - 1], at(lax.rem(me + k, 16)))
 
     def exchange_end(tile, slots, ssem, rsem, me):
@@ -285,6 +299,9 @@
             total = total + slots[k]
         return total
 
+    gathered = list(pending), list(later)
+    pending.clear()
+    later.clear()
     exchange_start(TT, TG1, as1, ar1, me_xy, at_xy)
 
     def factors(slab, cross_sum):
@@ -304,6 +321,14 @@
             CP[rr] = expd * slope
         return cross_sum
 
+    for copy in gathered[0]:
+        copy.wait_send()
+
+    @pl.when(c == 1)
+    def _():
+        for make in gathered[1]:
+            make().wait_send()
+
     turn(1, 0)
 
     def give(i):
@@ -413,7 +438,7 @@
     def _():
         arrived(H.at[3 * ROWS : 4 * ROWS], cs.at[1], cr.at[1])
 
-    head_chunks(0, 1)
+    head_chunks(0, 2)
     arrived(R1.at[3], q1s.at[3], q1r.at[3])
     arrived(R1.at[2], q1s.at[2], q1r.at[2])
     for n in range(4):
@@ -421,7 +446,7 @@
             second(k, n)
     CR2[...] = exchange_end(CR, CG1, bs1, br1, me_xy)
     exchange_start(CR2, CG2, bs2, br2, me_zc, at_zc)
-    head_chunks(1, 3)
+    head_chunks(2, 4)
 
     at_home = (c == 0) & (zl == 0)
     at_home_hi = (c == 0) & (zl == 1)
@@ -455,19 +480,12 @@
                 else:
                     to_owner(k, i, c_).start()
 
-    head_chunks(3, 7)
+    head_chunks(4, 7)
     cross = exchange_end(CR2, CG2, bs2, br2, me_zc)
     KL[0:4] = cross[0:4] / TOT[4:8] - jnp.log(TOT[4:8]) + jnp.log(TOT[0:4])
     kl_out[...] = KL[pl.ds(a, 1)]
 
-    for copy in pending:
-        copy.wait_send()
-
-    @pl.when(c == 1)
-    def _():
-        for make in later:
-            make().wait_send()
-
+    flush()
     for k, i, c_ in owners:
         if i == 0 and c_ == 0:
             home = at_home if k == 0 else at_home_hi

time: 71.3 us -> 70 us (0.982)
  Pallas kernels: 70.3 us -> 69.3 us
    pallas_call x1, Pallas kernels: 67.8 us -> 66.8 us  [on_device(): pl.pallas_call(kernel, out_shape=(vm((1, ROWS), F32), vm((56, ROWS), BF16...]
where the time goes in v5:
time: 70 us; the launch traced here: 69.9 us
  Pallas kernels  69.3 us (99%)
    pallas_call x1, Pallas kernels, on_device(): pl.pallas_call(kernel, out_shape=(vm((1, ROWS), F32), vm((56, ROWS), BF16...  66.8 us
    pallas_call x1, Pallas kernels, on_device(): pl.pallas_call(results, out_shape=(jax.ShapeDtypeStruct((1, ROWS), F32),...  2.48 us

profile of v5, /device:TPU:1, one launch (start us, length us, event | category | flops | bytes accessed | tf_op | source)
XLA Modules:
  0.0 69.9 jit_solution(6299790260235944332)
XLA Ops:
  0.6 66.8 %shard_map.67 = (f32[1,128]{1,0:T(1,128)S(1)}, bf16[56,128]{1,0:T(8,128)(2,1)S(1)}, bf16[750,3584]{1,0:T(8,128)(2,1)S(1)}) custom-call(bf16[128,3584]{1,0:T(8,128)(2,1)} %hid.1, s32[1,128]{1,0:T(1,128)} %bitcast.6, bf16[750,3584]{1,0:T(8,128)(2,1)} %head.1, bf16[3000,128]{1,0:T(8,128)(2,1)} %bitcast.4), custom_call_target="tpu_custom_call" | custom-call | flops 8257536000 | bytes 13000000 | tf_op jit(solution)/shard_map/pallas_call | solution.py:531
  67.4 2.5 %shard_map.68 = (f32[1,128]{1,0:T(1,128)}, bf16[56,128]{1,0:T(8,128)(2,1)}, bf16[750,3584]{1,0:T(8,128)(2,1)}) custom-call(f32[1,128]{1,0:T(1,128)S(1)} %get-tuple-element.9.kl, bf16[56,128]{1,0:T(8,128)(2,1)S(1)} %get-tuple-element.10.dhid, bf16[750,3584]{1,0:T(8,128)(2,1)S(1)} %get-tuple-element.11.dhead), custom_call_target="tpu_custom_call" | custom-call | tf_op jit(solution)/shard_map/pallas_call | solution.py:588

commit v6 on v5

--- a/solution.py
+++ b/solution.py
@@ -262,6 +262,7 @@
     logits(1, q, True)
     logits(1, before)
     logits(1, after)
+    turn(1, 0)
     passed(4, 0, across)
     passed(5, 1, across)
     in_slab = lax.broadcasted_iota(jnp.int32, (256, HALF), 0) < SLAB - 512
@@ -321,15 +322,7 @@
             CP[rr] = expd * slope
         return cross_sum
 
-    for copy in gathered[0]:
-        copy.wait_send()
-
-    @pl.when(c == 1)
-    def _():
-        for make in gathered[1]:
-            make().wait_send()
-
-    turn(1, 0)
+    turn(1, 1)
 
     def give(i):
         send(TR.at[2 * (1 - c) + i], TSIB.at[i], ts.at[4 + i], tr.at[4 + i], sib)
@@ -342,7 +335,6 @@
     arrived(TR.at[2], ts.at[3], tr.at[3])
     give(0)
     cross_sum = factors(0, jnp.zeros((1, HALF), F32))
-    turn(1, 1)
     for i in range(2):
         arrived(TSIB.at[i], ts.at[4 + i], tr.at[4 + i])
     cross_sum = factors(1, cross_sum)
@@ -437,6 +429,14 @@
     @pl.when(c == 0)
     def _():
         arrived(H.at[3 * ROWS : 4 * ROWS], cs.at[1], cr.at[1])
+
+    for copy in gathered[0]:
+        copy.wait_send()
+
+    @pl.when(c == 1)
+    def _():
+        for make in gathered[1]:
+            make().wait_send()
 
     head_chunks(0, 2)
     arrived(R1.at[3], q1s.at[3], q1r.at[3])

time: 70 us -> 70.6 us (level)
  no operation moved by 1% of the time
where the time goes in v6:
time: 70.6 us; the launch traced here: 70.5 us
  Pallas kernels  69.9 us (99%)
    pallas_call x1, Pallas kernels, on_device(): pl.pallas_call(kernel, out_shape=(vm((1, ROWS), F32), vm((56, ROWS), BF16...  67.4 us
    pallas_call x1, Pallas kernels, on_device(): pl.pallas_call(results, out_shape=(jax.ShapeDtypeStruct((1, ROWS), F32),...  2.48 us

profile of v6, /device:TPU:1, one launch (start us, length us, event | category | flops | bytes accessed | tf_op | source)
XLA Modules:
  0.0 70.5 jit_solution(13428648397275247287)
XLA Ops:
  0.6 67.4 %shard_map.67 = (f32[1,128]{1,0:T(1,128)S(1)}, bf16[56,128]{1,0:T(8,128)(2,1)S(1)}, bf16[750,3584]{1,0:T(8,128)(2,1)S(1)}) custom-call(bf16[128,3584]{1,0:T(8,128)(2,1)} %hid.1, s32[1,128]{1,0:T(1,128)} %bitcast.6, bf16[750,3584]{1,0:T(8,128)(2,1)} %head.1, bf16[3000,128]{1,0:T(8,128)(2,1)} %bitcast.4), custom_call_target="tpu_custom_call" | custom-call | flops 8257536000 | bytes 13000000 | tf_op jit(solution)/shard_map/pallas_call | solution.py:531
  68.0 2.5 %shard_map.68 = (f32[1,128]{1,0:T(1,128)}, bf16[56,128]{1,0:T(8,128)(2,1)}, bf16[750,3584]{1,0:T(8,128)(2,1)}) custom-call(f32[1,128]{1,0:T(1,128)S(1)} %get-tuple-element.9.kl, bf16[56,128]{1,0:T(8,128)(2,1)S(1)} %get-tuple-element.10.dhid, bf16[750,3584]{1,0:T(8,128)(2,1)S(1)} %get-tuple-element.11.dhead), custom_call_target="tpu_custom_call" | custom-call | tf_op jit(solution)/shard_map/pallas_call | solution.py:588

commit v7 on v5

--- a/solution.py
+++ b/solution.py
@@ -178,7 +178,8 @@
             while done < 256:
                 chip, row = divmod(n * 256 + done, CHIPCOL)
                 size = min(CHIPCOL - row, 256 - done)
-                HDT[half, chip // 4, chip % 4, row : row + size, slab * VP : (slab + 1) * VP] = out[done : done + size]
+                p_, q_ = jnp.where(c == 0, chip % 4, chip // 4), jnp.where(c == 0, chip // 4, chip % 4)
+                HDT[half, p_, q_, row : row + size, slab * VP : (slab + 1) * VP] = out[done : done + size]
                 done += size
 
     def piece(g, p_):
@@ -364,10 +365,8 @@
     up, down, far = mod4(p + 1), mod4(p - 1), mod4(p + 2)
 
     def partial(n, p_):
-        rows = []
-        for i in range(4):
-            rows.append(HDT[n, jnp.where(c == 0, i, p_), jnp.where(c == 0, p_, i)])
-        return jnp.dot(jnp.concatenate(rows, axis=0), GV[...], preferred_element_type=F32)
+        rows = HDT[n, p_].reshape(4 * CHIPCOL, 2 * VP)
+        return jnp.dot(rows, GV[...], preferred_element_type=F32)
 
     def put(ref, n, block):
         for i in range(4):
@@ -377,10 +376,10 @@
     send(B1.at[0], R1.at[0], q1s.at[0], q1r.at[0], at_p(up))
     put(B1, 1, partial(1, far))
     send(B1.at[1], R1.at[1], q1s.at[1], q1r.at[1], at_p(down))
+    put(B1, 2, partial(1, up))
+    send(B1.at[2], R1.at[2], q1s.at[2], q1r.at[2], at_p(up))
     put(B1, 3, partial(0, down))
     send(B1.at[3], R1.at[3], q1s.at[3], q1r.at[3], at_p(down))
-    put(B1, 2, partial(1, up))
-    send(B1.at[2], R1.at[2], q1s.at[2], q1r.at[2], at_p(up))
     send(GV.at[VP : 2 * VP], GTD.at[:, my_half], gs.at[0], gr.at[0], sib)
 
     def share(g):

time: 70 us -> 69.7 us (level)
  no operation moved by 1% of the time
where the time goes in v7:
time: 69.7 us
  Pallas kernels  69 us (99%)
    pallas_call x1, Pallas kernels, on_device(): pl.pallas_call(kernel, out_shape=(vm((1, ROWS), F32), vm((56, ROWS), BF16...  66.5 us
    pallas_call x1, Pallas kernels, on_device(): pl.pallas_call(results, out_shape=(jax.ShapeDtypeStruct((1, ROWS), F32),...  2.48 us

profile of v7, /device:TPU:1, one launch (start us, length us, event | category | flops | bytes accessed | tf_op | source)
XLA Modules:
  0.0 69.7 jit_solution(8843411034260632667)
XLA Ops:
  0.6 66.5 %shard_map.67 = (f32[1,128]{1,0:T(1,128)S(1)}, bf16[56,128]{1,0:T(8,128)(2,1)S(1)}, bf16[750,3584]{1,0:T(8,128)(2,1)S(1)}) custom-call(bf16[128,3584]{1,0:T(8,128)(2,1)} %hid.1, s32[1,128]{1,0:T(1,128)} %bitcast.6, bf16[750,3584]{1,0:T(8,128)(2,1)} %head.1, bf16[3000,128]{1,0:T(8,128)(2,1)} %bitcast.4), custom_call_target="tpu_custom_call" | custom-call | flops 8257536000 | bytes 13000000 | tf_op jit(solution)/shard_map/pallas_call | solution.py:530
  67.2 2.5 %shard_map.68 = (f32[1,128]{1,0:T(1,128)}, bf16[56,128]{1,0:T(8,128)(2,1)}, bf16[750,3584]{1,0:T(8,128)(2,1)}) custom-call(f32[1,128]{1,0:T(1,128)S(1)} %get-tuple-element.9.kl, bf16[56,128]{1,0:T(8,128)(2,1)S(1)} %get-tuple-element.10.dhid, bf16[750,3584]{1,0:T(8,128)(2,1)S(1)} %get-tuple-element.11.dhead), custom_call_target="tpu_custom_call" | custom-call | tf_op jit(solution)/shard_map/pallas_call | solution.py:587

commit v8 on v7

--- a/solution.py
+++ b/solution.py
@@ -445,7 +445,7 @@
             second(k, n)
     CR2[...] = exchange_end(CR, CG1, bs1, br1, me_xy)
     exchange_start(CR2, CG2, bs2, br2, me_zc, at_zc)
-    head_chunks(2, 4)
+    head_chunks(2, 5)
 
     at_home = (c == 0) & (zl == 0)
     at_home_hi = (c == 0) & (zl == 1)
@@ -479,7 +479,7 @@
                 else:
                     to_owner(k, i, c_).start()
 
-    head_chunks(4, 7)
+    head_chunks(5, 7)
     cross = exchange_end(CR2, CG2, bs2, br2, me_zc)
     KL[0:4] = cross[0:4] / TOT[4:8] - jnp.log(TOT[4:8]) + jnp.log(TOT[0:4])
     kl_out[...] = KL[pl.ds(a, 1)]

time: 69.7 us -> 70.1 us (level)
  no operation moved by 1% of the time
where the time goes in v8:
time: 70.1 us; the launch traced here: 69.8 us
  Pallas kernels  69.1 us (99%)
    pallas_call x1, Pallas kernels, on_device(): pl.pallas_call(kernel, out_shape=(vm((1, ROWS), F32), vm((56, ROWS), BF16...  66.7 us
    pallas_call x1, Pallas kernels, on_device(): pl.pallas_call(results, out_shape=(jax.ShapeDtypeStruct((1, ROWS), F32),...  2.48 us

profile of v8, /device:TPU:1, one launch (start us, length us, event | category | flops | bytes accessed | tf_op | source)
XLA Modules:
  0.0 69.8 jit_solution(11711576350571926847)
XLA Ops:
  0.6 66.7 %shard_map.67 = (f32[1,128]{1,0:T(1,128)S(1)}, bf16[56,128]{1,0:T(8,128)(2,1)S(1)}, bf16[750,3584]{1,0:T(8,128)(2,1)S(1)}) custom-call(bf16[128,3584]{1,0:T(8,128)(2,1)} %hid.1, s32[1,128]{1,0:T(1,128)} %bitcast.6, bf16[750,3584]{1,0:T(8,128)(2,1)} %head.1, bf16[3000,128]{1,0:T(8,128)(2,1)} %bitcast.4), custom_call_target="tpu_custom_call" | custom-call | flops 8257536000 | bytes 13000000 | tf_op jit(solution)/shard_map/pallas_call | solution.py:530
  67.3 2.5 %shard_map.68 = (f32[1,128]{1,0:T(1,128)}, bf16[56,128]{1,0:T(8,128)(2,1)}, bf16[750,3584]{1,0:T(8,128)(2,1)}) custom-call(f32[1,128]{1,0:T(1,128)S(1)} %get-tuple-element.9.kl, bf16[56,128]{1,0:T(8,128)(2,1)S(1)} %get-tuple-element.10.dhid, bf16[750,3584]{1,0:T(8,128)(2,1)S(1)} %get-tuple-element.11.dhead), custom_call_target="tpu_custom_call" | custom-call | tf_op jit(solution)/shard_map/pallas_call | solution.py:587

commit v9 on v7

--- a/solution.py
+++ b/solution.py
@@ -322,14 +322,6 @@
             CP[rr] = expd * slope
         return cross_sum
 
-    for copy in gathered[0]:
-        copy.wait_send()
-
-    @pl.when(c == 1)
-    def _():
-        for make in gathered[1]:
-            make().wait_send()
-
     turn(1, 0)
 
     def give(i):
@@ -478,6 +470,14 @@
                         RZ[z] = B3[k, 0, 0]
                 else:
                     to_owner(k, i, c_).start()
+
+    for copy in gathered[0]:
+        copy.wait_send()
+
+    @pl.when(c == 1)
+    def _():
+        for make in gathered[1]:
+            make().wait_send()
 
     head_chunks(4, 7)
     cross = exchange_end(CR2, CG2, bs2, br2, me_zc)

time: 69.7 us -> 69.8 us (level)
  no operation moved by 1% of the time
where the time goes in v9:
time: 69.8 us; the launch traced here: 69.7 us
  Pallas kernels  69 us (99%)
    pallas_call x1, Pallas kernels, on_device(): pl.pallas_call(kernel, out_shape=(vm((1, ROWS), F32), vm((56, ROWS), BF16...  66.6 us
    pallas_call x1, Pallas kernels, on_device(): pl.pallas_call(results, out_shape=(jax.ShapeDtypeStruct((1, ROWS), F32),...  2.48 us

profile of v9, /device:TPU:1, one launch (start us, length us, event | category | flops | bytes accessed | tf_op | source)
XLA Modules:
  0.0 69.7 jit_solution(7668661083191230050)
XLA Ops:
  0.6 66.6 %shard_map.67 = (f32[1,128]{1,0:T(1,128)S(1)}, bf16[56,128]{1,0:T(8,128)(2,1)S(1)}, bf16[750,3584]{1,0:T(8,128)(2,1)S(1)}) custom-call(bf16[128,3584]{1,0:T(8,128)(2,1)} %hid.1, s32[1,128]{1,0:T(1,128)} %bitcast.6, bf16[750,3584]{1,0:T(8,128)(2,1)} %head.1, bf16[3000,128]{1,0:T(8,128)(2,1)} %bitcast.4), custom_call_target="tpu_custom_call" | custom-call | flops 8257536000 | bytes 13000000 | tf_op jit(solution)/shard_map/pallas_call | solution.py:530
  67.2 2.5 %shard_map.68 = (f32[1,128]{1,0:T(1,128)}, bf16[56,128]{1,0:T(8,128)(2,1)}, bf16[750,3584]{1,0:T(8,128)(2,1)}) custom-call(f32[1,128]{1,0:T(1,128)S(1)} %get-tuple-element.9.kl, bf16[56,128]{1,0:T(8,128)(2,1)S(1)} %get-tuple-element.10.dhid, bf16[750,3584]{1,0:T(8,128)(2,1)S(1)} %get-tuple-element.11.dhead), custom_call_target="tpu_custom_call" | custom-call | tf_op jit(solution)/shard_map/pallas_call | solution.py:587
